TPU v7x, 32 devices: a whole 2x2x4 slice. The times are simulated.
32 devices in a mesh: dp: 8 (over z, y), mp: 4 (over x, core).
Axes of the slice: x: 2, y: 2, z: 4, core: 2. Of those that a mesh axis runs over, the one named last changes fastest.
Arguments:
- tokens: bfloat16 [1536, 1152], P('dp'), may hold values from -6 to 6
- doc_lengths: int32 [16, 2], P('dp'), may hold values from 1 to 48, as said below
- cotangent: bfloat16 [1536, 1152], P('dp'), may hold values from -6 to 6
- query_weight: bfloat16 [1152, 1024], P('dp', 'mp'), may hold values from -0.1875 to 0.1875
- key_weight: bfloat16 [1152, 256], P('dp'), may hold values from -0.1875 to 0.1875
- value_weight: bfloat16 [1152, 256], P('dp'), may hold values from -0.1875 to 0.1875
- out_weight: bfloat16 [1024, 1152], P('mp', 'dp'), may hold values from -0.1875 to 0.1875
- gate_weight: bfloat16 [1152, 6912], P('dp', 'mp'), may hold values from -0.1875 to 0.1875
- up_weight: bfloat16 [1152, 6912], P('dp', 'mp'), may hold values from -0.1875 to 0.1875
- down_weight: bfloat16 [6912, 1152], P('mp', 'dp'), may hold values from -0.078125 to 0.078125
- pre_attn_gain: bfloat16 [1152], P('dp'), may hold values from 0.5 to 1.5
- post_attn_gain: bfloat16 [1152], P('dp'), may hold values from 0.5 to 1.5
- pre_ffn_gain: bfloat16 [1152], P('dp'), may hold values from 0.5 to 1.5
- post_ffn_gain: bfloat16 [1152], P('dp'), may hold values from 0.5 to 1.5
- query_gain: bfloat16 [256], P('dp'), may hold values from 0.5 to 1.5
- key_gain: bfloat16 [256], P('dp'), may hold values from 0.5 to 1.5
Outputs:
- mixed: bfloat16 [1536, 1152], P('dp')
- tokens_grad: float32 [1536, 1152], P('dp')
- query_grad: float32 [1152, 1024], P('dp', 'mp')
- key_grad: float32 [1152, 256], P('dp')
- value_grad: float32 [1152, 256], P('dp')
- out_grad: float32 [1024, 1152], P('mp', 'dp')
- gate_grad: float32 [1152, 6912], P('dp', 'mp')
- up_grad: float32 [1152, 6912], P('dp', 'mp')
- down_grad: float32 [6912, 1152], P('mp', 'dp')
- pre_attn_grad: float32 [1152], P('dp')
- post_attn_grad: float32 [1152], P('dp')
- pre_ffn_grad: float32 [1152], P('dp')
- post_ffn_grad: float32 [1152], P('dp')
- query_gain_grad: float32 [256], P('dp')
- key_gain_grad: float32 [256], P('dp')
Inputs may be any that keep to these rules, and one draw needn't show every extreme that they name: Row b of doc_lengths gives the 2 document lengths of buffer b, the buffers of one index of dp being 2 consecutive rows; the documents lie end to end from the buffer's first row, and the rows after them are padding.
All inputs are finite; a program needn't handle non-finite values.
Results may differ from a plain program's by a relative error of at most 0.019.
Values may be sent and summed in bfloat16 or wider, within the bound.
A program may use at most 128 MiB of HBM per device.

v0:
```python
import jax
import jax.numpy as jnp
from jax import lax
from jax.sharding import PartitionSpec as P

WINDOW = 512


EPSILON = 1e-06
THETA_BASE = 10000.0
NEGATIVE = -1e30


def matmul(left_op, right_op):
    return jnp.dot(left_op, right_op, preferred_element_type=jnp.float32)


def inner_rows(left_op, right_op):
    return lax.dot_general(
        left_op, right_op, (((0,), (0,)), ((), ())), preferred_element_type=jnp.float32
    )


def inner_cols(left_op, right_op):
    return lax.dot_general(
        left_op, right_op, (((1,), (1,)), ((), ())), preferred_element_type=jnp.float32
    )


def normed(values, factor):
    return values * lax.rsqrt(jnp.mean(values * values, axis=-1, keepdims=True) + EPSILON) * factor


def rotate(values, cosine, sine_table):
    half_width = values.shape[-1] // 2
    leading = values[..., :half_width]
    trailing = values[..., half_width:]
    return jnp.concatenate(
        [leading * cosine - trailing * sine_table, trailing * cosine + leading * sine_table],
        axis=-1,
    )


def layout(lengths, row_count):
    doc_ends = jnp.cumsum(lengths)
    row_index = jnp.arange(row_count, dtype=jnp.int32)
    passed = row_index[:, None] >= doc_ends[None, :]
    segment = jnp.sum(passed.astype(jnp.int32), axis=1)
    begins = jnp.sum(jnp.where(passed, lengths[None, :], 0), axis=1)
    position = row_index - begins
    live_rows = (segment < lengths.shape[0]).astype(jnp.float32)
    allowed = (
        (segment[:, None] == segment[None, :])
        & (row_index[None, :] <= row_index[:, None])
        & (row_index[:, None] - row_index[None, :] < WINDOW)
    )
    return (position, live_rows, allowed)


def angles(position, head_width):
    half_width = head_width // 2
    frequency = THETA_BASE ** (-2.0 * jnp.arange(half_width, dtype=jnp.float32) / head_width)
    turned = position.astype(jnp.float32)[:, None] * frequency[None, :]
    return (jnp.cos(turned), jnp.sin(turned))


def attention_front(inputs, lengths, gathered):
    (
        query_w,
        key_w,
        value_w,
        out_w,
        gate_w,
        up_w,
        down_w,
        gain_one,
        gain_two,
        gain_three,
        gain_four,
        query_g,
        key_g,
    ) = gathered
    head_width = query_w.shape[1]
    position, live_rows, allowed = layout(lengths, inputs.shape[0])
    cosine, sine_table = angles(position, head_width)
    normed_in = normed(inputs, gain_one).astype(jnp.bfloat16)
    query_pre = matmul(normed_in, query_w)
    key_pre = matmul(normed_in, key_w)
    value_low = matmul(normed_in, value_w).astype(jnp.bfloat16)
    query_low = rotate(normed(query_pre, query_g), cosine, sine_table).astype(jnp.bfloat16)
    key_low = rotate(normed(key_pre, key_g), cosine, sine_table).astype(jnp.bfloat16)
    scores = inner_cols(query_low, key_low) * head_width ** (-0.5)
    scores = jnp.where(allowed, scores, NEGATIVE)
    row_peak = jnp.max(scores, axis=1, keepdims=True)
    raised = jnp.exp(scores - row_peak)
    attention = raised / jnp.sum(raised, axis=1, keepdims=True)
    attended = matmul(attention.astype(jnp.bfloat16), value_low).astype(jnp.bfloat16)
    return (
        normed_in,
        query_pre,
        key_pre,
        value_low,
        query_low,
        key_low,
        attention,
        attended,
        live_rows,
        cosine,
        sine_table,
    )


def ffn_front(middle, gathered):
    normed_mid = normed(middle, gathered[9]).astype(jnp.bfloat16)
    gate_proj = matmul(normed_mid, gathered[4])
    up_proj = matmul(normed_mid, gathered[5])
    hidden = (jax.nn.gelu(gate_proj, approximate=True) * up_proj).astype(jnp.bfloat16)
    return (normed_mid, gate_proj, up_proj, hidden)


def forward_pass(inputs, lengths, gathered):
    front = attention_front(inputs, lengths, gathered)
    attended = front[7]
    live_rows = front[8]
    attn_part = lax.psum_scatter(
        matmul(attended, gathered[3]), "mp", scatter_dimension=0, tiled=True
    )
    attn_sum = lax.all_gather(attn_part, "mp", axis=0, tiled=True)
    middle = inputs + normed(attn_sum, gathered[8]) * live_rows[:, None]
    normed_mid, gate_proj, up_proj, hidden = ffn_front(middle, gathered)
    ffn_part = lax.psum_scatter(matmul(hidden, gathered[6]), "mp", scatter_dimension=0, tiled=True)
    ffn_sum = lax.all_gather(ffn_part, "mp", axis=0, tiled=True)
    output = middle + normed(ffn_sum, gathered[10]) * live_rows[:, None]
    return (output, attn_sum, ffn_sum)


def backward_pass(inputs, lengths, upstream, attn_sum, ffn_sum, gathered):
    (
        query_w,
        key_w,
        value_w,
        out_w,
        gate_w,
        up_w,
        down_w,
        gain_one,
        gain_two,
        gain_three,
        gain_four,
        query_g,
        key_g,
    ) = gathered
    (
        normed_in,
        query_pre,
        key_pre,
        value_low,
        query_low,
        key_low,
        attention,
        attended,
        live_rows,
        cosine,
        sine_table,
    ) = attention_front(inputs, lengths, gathered)
    head_width = query_w.shape[1]
    middle = inputs + normed(attn_sum, gain_two) * live_rows[:, None]
    normed_mid, gate_proj, up_proj, hidden = ffn_front(middle, gathered)
    _, back_four = jax.vjp(
        lambda values, factor: normed(values, factor) * live_rows[:, None], ffn_sum, gain_four
    )
    d_ffn, grad_four = back_four(upstream)
    d_ffn_low = d_ffn.astype(jnp.bfloat16)
    grad_down = inner_rows(hidden, d_ffn_low)
    d_hidden = inner_cols(d_ffn_low, down_w)
    _, back_glu = jax.vjp(
        lambda gate_in, up_in: jax.nn.gelu(gate_in, approximate=True) * up_in, gate_proj, up_proj
    )
    d_gate, d_up = back_glu(d_hidden)
    d_gate_low = d_gate.astype(jnp.bfloat16)
    d_up_low = d_up.astype(jnp.bfloat16)
    grad_gate = inner_rows(normed_mid, d_gate_low)
    grad_up = inner_rows(normed_mid, d_up_low)
    d_mid_part = inner_cols(d_gate_low, gate_w) + inner_cols(d_up_low, up_w)
    d_mid_share = lax.psum_scatter(d_mid_part, "mp", scatter_dimension=0, tiled=True)
    d_mid_norm = lax.all_gather(d_mid_share, "mp", axis=0, tiled=True)
    _, back_three = jax.vjp(lambda values, factor: normed(values, factor), middle, gain_three)
    d_mid_add, grad_three = back_three(d_mid_norm)
    d_middle = upstream + d_mid_add
    _, back_two = jax.vjp(
        lambda values, factor: normed(values, factor) * live_rows[:, None], attn_sum, gain_two
    )
    d_attn, grad_two = back_two(d_middle)
    d_attn_low = d_attn.astype(jnp.bfloat16)
    grad_out = inner_rows(attended, d_attn_low)
    d_attended = inner_cols(d_attn_low, out_w).astype(jnp.bfloat16)
    d_value = inner_rows(attention.astype(jnp.bfloat16), d_attended).astype(jnp.bfloat16)
    d_probs = inner_cols(d_attended, value_low)
    d_scores = attention * (d_probs - jnp.sum(attention * d_probs, axis=1, keepdims=True))
    d_scores_low = d_scores.astype(jnp.bfloat16)
    score_scale = head_width ** (-0.5)
    d_query_rot = matmul(d_scores_low, key_low) * score_scale
    d_key_rot = inner_rows(d_scores_low, query_low) * score_scale
    _, back_query = jax.vjp(
        lambda values, factor: rotate(normed(values, factor), cosine, sine_table),
        query_pre,
        query_g,
    )
    d_query_pre, grad_qgain = back_query(d_query_rot)
    _, back_key = jax.vjp(
        lambda values, factor: rotate(normed(values, factor), cosine, sine_table), key_pre, key_g
    )
    d_key_pre, grad_kgain = back_key(d_key_rot)
    d_query_low = d_query_pre.astype(jnp.bfloat16)
    d_key_low = d_key_pre.astype(jnp.bfloat16)
    grad_query = inner_rows(normed_in, d_query_low)
    grad_key = inner_rows(normed_in, d_key_low)
    grad_value = inner_rows(normed_in, d_value)
    d_in_part = (
        inner_cols(d_query_low, query_w)
        + inner_cols(d_key_low, key_w)
        + inner_cols(d_value, value_w)
    )
    d_in_share = lax.psum_scatter(
        d_in_part.astype(jnp.bfloat16), "mp", scatter_dimension=0, tiled=True
    ).astype(jnp.float32)
    d_in_norm = lax.all_gather(d_in_share.astype(jnp.bfloat16), "mp", axis=0, tiled=True).astype(
        d_in_share.dtype
    )
    _, back_one = jax.vjp(lambda values, factor: normed(values, factor), inputs, gain_one)
    d_in_add, grad_one = back_one(d_in_norm)
    d_inputs = d_middle + d_in_add
    grads = (
        grad_query,
        grad_key,
        grad_value,
        grad_out,
        grad_gate,
        grad_up,
        grad_down,
        grad_one,
        grad_two,
        grad_three,
        grad_four,
        grad_qgain,
        grad_kgain,
    )
    return (d_inputs, grads)


def widened(gathered):
    return gathered[:7] + tuple((member.astype(jnp.float32) for member in gathered[7:]))


def summed(former, latter):
    if former is None:
        return latter
    return jax.tree.map(lambda first, second: first + second, former, latter)


def on_device(
    tokens,
    doc_lengths,
    cotangent,
    query_weight,
    key_weight,
    value_weight,
    out_weight,
    gate_weight,
    up_weight,
    down_weight,
    pre_attn_gain,
    post_attn_gain,
    pre_ffn_gain,
    post_ffn_gain,
    query_gain,
    key_gain,
):
    batches = doc_lengths.shape[0]
    rows_here = tokens.shape[0] // batches
    outputs = []
    input_grads = []
    totals = None
    owned = None
    for batch_index in range(batches):
        row_start = batch_index * rows_here
        inputs = tokens[row_start : row_start + rows_here].astype(jnp.float32)
        upstream = cotangent[row_start : row_start + rows_here].astype(jnp.float32)
        lengths = doc_lengths[batch_index]
        forward_set = widened(
            (
                lax.all_gather(query_weight, "dp", axis=0, tiled=True),
                lax.all_gather(key_weight, "dp", axis=0, tiled=True),
                lax.all_gather(value_weight, "dp", axis=0, tiled=True),
                lax.all_gather(out_weight, "dp", axis=1, tiled=True),
                lax.all_gather(gate_weight, "dp", axis=0, tiled=True),
                lax.all_gather(up_weight, "dp", axis=0, tiled=True),
                lax.all_gather(down_weight, "dp", axis=1, tiled=True),
                lax.all_gather(pre_attn_gain, "dp", axis=0, tiled=True),
                lax.all_gather(post_attn_gain, "dp", axis=0, tiled=True),
                lax.all_gather(pre_ffn_gain, "dp", axis=0, tiled=True),
                lax.all_gather(post_ffn_gain, "dp", axis=0, tiled=True),
                lax.all_gather(query_gain, "dp", axis=0, tiled=True),
                lax.all_gather(key_gain, "dp", axis=0, tiled=True),
            )
        )
        output, attn_sum, ffn_sum = forward_pass(inputs, lengths, forward_set)
        backward_set = widened(
            (
                lax.all_gather(query_weight, "dp", axis=0, tiled=True),
                lax.all_gather(key_weight, "dp", axis=0, tiled=True),
                lax.all_gather(value_weight, "dp", axis=0, tiled=True),
                lax.all_gather(out_weight, "dp", axis=1, tiled=True),
                lax.all_gather(gate_weight, "dp", axis=0, tiled=True),
                lax.all_gather(up_weight, "dp", axis=0, tiled=True),
                lax.all_gather(down_weight, "dp", axis=1, tiled=True),
                lax.all_gather(pre_attn_gain, "dp", axis=0, tiled=True),
                lax.all_gather(post_attn_gain, "dp", axis=0, tiled=True),
                lax.all_gather(pre_ffn_gain, "dp", axis=0, tiled=True),
                lax.all_gather(post_ffn_gain, "dp", axis=0, tiled=True),
                lax.all_gather(query_gain, "dp", axis=0, tiled=True),
                lax.all_gather(key_gain, "dp", axis=0, tiled=True),
            )
        )
        d_inputs, grads = backward_pass(inputs, lengths, upstream, attn_sum, ffn_sum, backward_set)
        outputs.append(output.astype(jnp.bfloat16))
        input_grads.append(d_inputs)
        totals = summed(totals, grads)
    owned = (
        lax.psum_scatter(totals[0], "dp", scatter_dimension=0, tiled=True),
        lax.psum_scatter(totals[1], "dp", scatter_dimension=0, tiled=True),
        lax.psum_scatter(totals[2], "dp", scatter_dimension=0, tiled=True),
        lax.psum_scatter(totals[3], "dp", scatter_dimension=1, tiled=True),
        lax.psum_scatter(totals[4], "dp", scatter_dimension=0, tiled=True),
        lax.psum_scatter(totals[5], "dp", scatter_dimension=0, tiled=True),
        lax.psum_scatter(totals[6], "dp", scatter_dimension=1, tiled=True),
        lax.psum_scatter(totals[7], "dp", scatter_dimension=0, tiled=True),
        lax.psum_scatter(totals[8], "dp", scatter_dimension=0, tiled=True),
        lax.psum_scatter(totals[9], "dp", scatter_dimension=0, tiled=True),
        lax.psum_scatter(totals[10], "dp", scatter_dimension=0, tiled=True),
        lax.psum_scatter(totals[11], "dp", scatter_dimension=0, tiled=True),
        lax.psum_scatter(totals[12], "dp", scatter_dimension=0, tiled=True),
    )
    shared_heads = lax.psum((owned[1], owned[2], owned[11], owned[12]), "mp")
    mixed = jnp.concatenate(outputs, axis=0)
    tokens_grad = jnp.concatenate(input_grads, axis=0)
    return (
        mixed,
        tokens_grad,
        owned[0],
        shared_heads[0],
        shared_heads[1],
        owned[3],
        owned[4],
        owned[5],
        owned[6],
        owned[7],
        owned[8],
        owned[9],
        owned[10],
        shared_heads[2],
        shared_heads[3],
    )


def solution(mesh):
    placed = (
        P("dp", None),
        P("dp", None),
        P("dp", None),
        P("dp", "mp"),
        P("dp", None),
        P("dp", None),
        P("mp", "dp"),
        P("dp", "mp"),
        P("dp", "mp"),
        P("mp", "dp"),
        P("dp"),
        P("dp"),
        P("dp"),
        P("dp"),
        P("dp"),
        P("dp"),
    )
    return jax.shard_map(
        on_device,
        mesh=mesh,
        in_specs=placed,
        out_specs=(
            P("dp", None),
            P("dp", None),
            P("dp", "mp"),
            P("dp", None),
            P("dp", None),
            P("mp", "dp"),
            P("dp", "mp"),
            P("dp", "mp"),
            P("mp", "dp"),
            P("dp"),
            P("dp"),
            P("dp"),
            P("dp"),
            P("dp"),
            P("dp"),
        ),
        check_vma=False,
    )
```

profile of v0, /device:TPU:13, one launch (start us, length us, event | category | flops | bytes accessed | tf_op | source)
XLA Modules:
  0.0 1303.4 jit_solution(18399920917020185031)
XLA Ops:
  15.8 23.3 %all-reduce.31 = (bf16[1152]{0:T(1024)(128)(2,1)S(1)}, bf16[256]{0:T(256)(128)(2,1)S(1)}, bf16[256]{0:T(256)(128)(2,1)S(1)}, bf16[1152]{0:T(1024)(128)(2,1)S(1)}...) all-reduce(bf16[1152]{0:T(1024)(128)(2,1)S(1)} %dynamic-update-slic, ...), channel_id=1, replica_groups=mesh['dp'=8,'mp'=4] {'dp'}, use_global_device_ids=true, to_apply=%add.8 | all-reduce | flops 5120 | bytes 20480
  40.4 26.0 %all_gather.45 = bf16[1152,256]{1,0:T(8,128)(2,1)S(1)} all-gather(bf16[144,256]{1,0:T(8,128)(2,1)} %param.20), channel_id=1, replica_groups=mesh['dp'=8,'mp'=4] {'dp'}, dimensions={0}, use_global_device_ids=true | all-gather | bytes 663552 | tf_op jit(solution)/shard_map/all_gather | solution.py:293
  69.4 25.8 %all_gather.43 = bf16[1152,256]{1,0:T(8,128)(2,1)S(1)} all-gather(bf16[144,256]{1,0:T(8,128)(2,1)} %param.19), channel_id=1, replica_groups=mesh['dp'=8,'mp'=4] {'dp'}, dimensions={0}, use_global_device_ids=true | all-gather | bytes 663552 | tf_op jit(solution)/shard_map/all_gather | solution.py:292
  97.8 24.3 %all_gather.47 = bf16[1152,256]{1,0:T(8,128)(2,1)S(1)} all-gather(bf16[144,256]{1,0:T(8,128)(2,1)S(1)} %copy-done.74), channel_id=1, replica_groups=mesh['dp'=8,'mp'=4] {'dp'}, dimensions={0}, use_global_device_ids=true | all-gather | bytes 663552 | tf_op jit(solution)/shard_map/all_gather | solution.py:294
  122.4 26.6 %all_gather.48 = bf16[256,1152]{0,1:T(8,128)(2,1)S(1)} all-gather(bf16[256,144]{0,1:T(8,128)(2,1)S(1)} %copy-done.75), channel_id=1, replica_groups=mesh['dp'=8,'mp'=4] {'dp'}, dimensions={1}, use_global_device_ids=true | all-gather | bytes 663552 | tf_op jit(solution)/shard_map/all_gather | solution.py:295
  155.5 52.1 %reduce-scatter.50.cloned.1.call-done = f32[24,1152]{1,0:T(8,128)} async-done(((f32[96,1152]{1,0:T(8,128)}), f32[24,1152]{1,0:T(8,128)}) %reduce-scatter.50.cloned.1.call-update) | async-done | bytes 110608
  207.5 7.0 all_gather.57
  214.7 17.1 %reduce-scatter.46.cloned.1.call-done = f32[24,1152]{1,0:T(8,128)} async-done(((f32[96,1152]{1,0:T(8,128)}), f32[24,1152]{1,0:T(8,128)}) %reduce-scatter.46.cloned.1.call-update) | async-done | bytes 110608
  231.8 7.0 all_gather.49
  240.3 19.8 %all-gather.4.cloned.1.call-done = bf16[1152,1728]{1,0:T(8,128)(2,1)} async-done(((bf16[144,1728]{1,0:T(8,128)(2,1)}), bf16[1152,1728]{1,0:T(8,128)(2,1)}) %all-gather.4.cloned.1.call-update) | async-done | bytes 3981328 | tf_op jit(solution)/shard_map/all_gather | solution.py:296
  260.1 3.8 fusion.175
  264.0 68.8 %all-gather.6.cloned.1.call-done = bf16[1152,1728]{1,0:T(8,128)(2,1)} async-done(((bf16[144,1728]{1,0:T(8,128)(2,1)}), bf16[1152,1728]{1,0:T(8,128)(2,1)}) %all-gather.6.cloned.1.call-update) | async-done | bytes 3981328 | tf_op jit(solution)/shard_map/all_gather | solution.py:297
  332.8 4.2 multiply_convert_fusion.2
  336.9 68.5 %all-gather.8.cloned.1.call-done = bf16[1728,1152]{0,1:T(8,128)(2,1)} async-done(((bf16[1728,144]{0,1:T(8,128)(2,1)}), bf16[1728,1152]{0,1:T(8,128)(2,1)}) %all-gather.8.cloned.1.call-update) | async-done | bytes 3981328 | tf_op jit(solution)/shard_map/all_gather | solution.py:298
  405.4 4.4 fusion.176
  409.9 3.1 fusion.172
  416.0 2.1 fusion.173
  418.3 14.1 %reduce-scatter.52.cloned.1.call-done = f32[24,1152]{1,0:T(8,128)} async-done(((f32[96,1152]{1,0:T(8,128)}), f32[24,1152]{1,0:T(8,128)}) %reduce-scatter.52.cloned.1.call-update) | async-done | bytes 110608
  432.4 7.0 all_gather.58
  440.6 15.8 %reduce-scatter.48.cloned.1.call-done = f32[24,1152]{1,0:T(8,128)} async-done(((f32[96,1152]{1,0:T(8,128)}), f32[24,1152]{1,0:T(8,128)}) %reduce-scatter.48.cloned.1.call-update) | async-done | bytes 110608
  456.4 7.2 all_gather.55
  464.4 3.0 fusion.35
  468.8 3.7 multiply_convert_fusion
  475.0 2.2 convolution_add_fusion.9
  478.6 3.9 multiply_convert_fusion.1
  484.9 2.2 convolution_add_fusion.12
  487.1 11.2 reduce-scatter.58.cloned.1.call-done
  498.3 7.8 all_gather.121
  506.2 16.3 %reduce-scatter.54.cloned.1.call-done = f32[24,1152]{1,0:T(8,128)} async-done(((f32[96,1152]{1,0:T(8,128)}), f32[24,1152]{1,0:T(8,128)}) %reduce-scatter.54.cloned.1.call-update) | async-done | bytes 110608
  522.5 7.2 all_gather.59
  532.8 2.4 multiply_reduce_fusion.3
  555.4 2.3 convolution_add_fusion.3
  559.9 5.6 fusion.145
  565.5 35.8 %reduce-scatter.36.cloned.1.call-done = f32[144,256]{1,0:T(8,128)} async-done(((f32[1152,256]{1,0:T(8,128)}), f32[144,256]{1,0:T(8,128)}) %reduce-scatter.36.cloned.1.call-update) | async-done | bytes 147472 | tf_op jit(solution)/shard_map/reduce_scatter | solution.py:332
  601.2 66.7 %reduce-scatter.34.cloned.1.call-done = f32[144,256]{1,0:T(8,128)} async-done(((f32[1152,256]{1,0:T(8,128)}), f32[144,256]{1,0:T(8,128)}) %reduce-scatter.34.cloned.1.call-update) | async-done | bytes 147472 | tf_op jit(solution)/shard_map/reduce_scatter | solution.py:331
  668.0 7.9 convolution_add_fusion
  678.3 4.5 convolution_add_fusion.1
  685.1 4.5 convolution_add_fusion.2
  692.1 8.6 all_gather.122
  700.8 12.3 reduce-scatter.56.cloned.1.call-done
  713.0 6.5 all_gather.120
  720.0 24.5 %all-reduce.28 = (f32[1152]{0:T(1024)S(1)}, f32[1152]{0:T(1024)S(1)}, f32[1152]{0:T(1024)S(1)}, f32[1152]{0:T(1024)S(1)}, f32[256]{0:T(256)S(1)}, /*index=5*/f32[256]{0:T(256)S(1)}) all-reduce(f32[1152]{0:T(1024)S(1)} %add.370, f32[1152]{0:T(1024)S(1)} %add.371, f32[1152]{0:T(1024)S(1)} %add.372, ...), channel_id=17, replica_groups=mesh['dp'=8,'mp'=4] {'dp'}, use_global_device_ids=true, to_apply=%region_55.56.clone | all-reduce | flops 5120 | bytes 40960
  747.2 11.8 all-reduce.29
  760.3 18.9 %reduce-scatter.38.cloned.1.call-done = f32[256,144]{0,1:T(8,128)} async-done(((f32[256,1152]{0,1:T(8,128)}), f32[256,144]{0,1:T(8,128)}) %reduce-scatter.38.cloned.1.call-update) | async-done | bytes 147472 | tf_op jit(solution)/shard_map/reduce_scatter | solution.py:333
  779.2 67.1 %reduce-scatter.32.cloned.1.call-done = f32[144,256]{1,0:T(8,128)} async-done(((f32[1152,256]{1,0:T(8,128)}), f32[144,256]{1,0:T(8,128)}) %reduce-scatter.32.cloned.1.call-update) | async-done | bytes 147472 | tf_op jit(solution)/shard_map/reduce_scatter | solution.py:330
  846.3 149.3 %reduce-scatter.44.cloned.1.call-done = f32[1728,144]{0,1:T(8,128)} async-done(((f32[1728,1152]{0,1:T(8,128)}), f32[1728,144]{0,1:T(8,128)}) %reduce-scatter.44.cloned.1.call-update) | async-done | bytes 995344 | tf_op jit(solution)/shard_map/reduce_scatter | solution.py:336
  995.7 148.5 %reduce-scatter.42.cloned.1.call-done = f32[144,1728]{1,0:T(8,128)} async-done(((f32[1152,1728]{1,0:T(8,128)}), f32[144,1728]{1,0:T(8,128)}) %reduce-scatter.42.cloned.1.call-update) | async-done | bytes 995344 | tf_op jit(solution)/shard_map/reduce_scatter | solution.py:335
  1144.2 148.6 %reduce-scatter.40.cloned.1.call-done = f32[144,1728]{1,0:T(8,128)} async-done(((f32[1152,1728]{1,0:T(8,128)}), f32[144,1728]{1,0:T(8,128)}) %reduce-scatter.40.cloned.1.call-update) | async-done | bytes 995344 | tf_op jit(solution)/shard_map/reduce_scatter | solution.py:334
  (477 shorter events, 71.0 us)
Async XLA Ops:
  8.0 88.8 %copy-start.5 = (bf16[192,1152]{1,0:T(8,128)(2,1)S(1)}, bf16[192,1152]{1,0:T(8,128)(2,1)}, u32[]{:S(2)}) copy-start(bf16[192,1152]{1,0:T(8,128)(2,1)} %param.16) | copy-start | bytes 1327108
  8.0 89.3 %copy-start.127 = (s32[2,2]{1,0:T(2,128)S(1)}, s32[2,2]{1,0:T(2,128)}, u32[]{:S(2)}) copy-start(s32[2,2]{1,0:T(2,128)} %param.17) | copy-start | bytes 52
  8.0 89.8 %copy-start.74 = (bf16[144,256]{1,0:T(8,128)(2,1)S(1)}, bf16[144,256]{1,0:T(8,128)(2,1)}, u32[]{:S(2)}) copy-start(bf16[144,256]{1,0:T(8,128)(2,1)} %param.21) | copy-start | bytes 221188
  8.0 114.3 %copy-start.75 = (bf16[256,144]{0,1:T(8,128)(2,1)S(1)}, bf16[256,144]{0,1:T(8,128)(2,1)}, u32[]{:S(2)}) copy-start(bf16[256,144]{0,1:T(8,128)(2,1)} %param.22) | copy-start | bytes 221188
  8.1 199.5 %reduce-scatter.50.cloned.1.call-start = ((), (), s32[]{:S(2)}) async-start(), calls=%async_computation.27 | async-start | bytes 552960
  40.4 108.6 %copy-start.128 = (f32[96]{0:T(128)}, f32[96]{0:T(128)S(1)}, u32[]{:S(2)}) copy-start(f32[96]{0:T(128)S(1)} %get-tuple-element.35) | copy-start | bytes 1156
  40.4 108.9 %copy-start.130 = (f32[96]{0:T(128)}, f32[96]{0:T(128)S(1)}, u32[]{:S(2)}) copy-start(f32[96]{0:T(128)S(1)} %get-tuple-element.36) | copy-start | bytes 1156
  40.4 111.6 %copy-start.81 = (f32[96]{0:T(128)}, f32[96]{0:T(128)S(1)}, u32[]{:S(2)}) copy-start(f32[96]{0:T(128)S(1)} %fusion.120) | copy-start | bytes 1156
  150.0 88.9 %copy-start.58 = (bf16[96,128]{1,0:T(8,128)(2,1)}, bf16[96,128]{1,0:T(8,128)(2,1)S(1)}, u32[]{:S(2)}) copy-start(bf16[96,128]{1,0:T(8,128)(2,1)S(1)} %get-tuple-element.92) | copy-start | bytes 73732
  150.0 88.8 %copy-start.60 = (bf16[96,128]{1,0:T(8,128)(2,1)}, bf16[96,128]{1,0:T(8,128)(2,1)S(1)}, u32[]{:S(2)}) copy-start(bf16[96,128]{1,0:T(8,128)(2,1)S(1)} %get-tuple-element.93) | copy-start | bytes 73732
  150.1 88.8 %copy-start.62 = (bf16[96,128]{1,0:T(8,128)(2,1)}, bf16[96,128]{1,0:T(8,128)(2,1)S(1)}, u32[]{:S(2)}) copy-start(bf16[96,128]{1,0:T(8,128)(2,1)S(1)} %get-tuple-element.118) | copy-start | bytes 73732
  150.1 88.8 %copy-start.64 = (bf16[96,128]{1,0:T(8,128)(2,1)}, bf16[96,128]{1,0:T(8,128)(2,1)S(1)}, u32[]{:S(2)}) copy-start(bf16[96,128]{1,0:T(8,128)(2,1)S(1)} %get-tuple-element.119) | copy-start | bytes 73732
  150.1 88.8 %copy-start.66 = (bf16[96,128]{1,0:T(8,128)(2,1)}, bf16[96,128]{1,0:T(8,128)(2,1)S(1)}, u32[]{:S(2)}) copy-start(bf16[96,128]{1,0:T(8,128)(2,1)S(1)} %get-tuple-element.136) | copy-start | bytes 73732
  150.1 88.8 %copy-start.68 = (bf16[96,128]{1,0:T(8,128)(2,1)}, bf16[96,128]{1,0:T(8,128)(2,1)S(1)}, u32[]{:S(2)}) copy-start(bf16[96,128]{1,0:T(8,128)(2,1)S(1)} %get-tuple-element.137) | copy-start | bytes 73732
  150.1 88.8 %copy-start.70 = (bf16[96,128]{1,0:T(8,128)(2,1)}, bf16[96,128]{1,0:T(8,128)(2,1)S(1)}, u32[]{:S(2)}) copy-start(bf16[96,128]{1,0:T(8,128)(2,1)S(1)} %get-tuple-element.138) | copy-start | bytes 73732
  150.1 88.8 %copy-start.72 = (bf16[96,128]{1,0:T(8,128)(2,1)}, bf16[96,128]{1,0:T(8,128)(2,1)S(1)}, u32[]{:S(2)}) copy-start(bf16[96,128]{1,0:T(8,128)(2,1)S(1)} %get-tuple-element.139) | copy-start | bytes 73732
  150.3 88.8 %copy-start.56 = (f32[96,96]{0,1:T(8,128)}, f32[96,96]{0,1:T(8,128)S(1)}, u32[]{:S(2)}) copy-start(f32[96,96]{0,1:T(8,128)S(1)} %get-tuple-element.151) | copy-start | bytes 110596
  150.3 88.8 %copy-start.114 = (f32[96]{0:T(128)}, f32[96]{0:T(128)S(1)}, u32[]{:S(2)}) copy-start(f32[96]{0:T(128)S(1)} %get-tuple-element.150) | copy-start | bytes 1156
  150.4 88.7 %copy-start.116 = (f32[96]{0:T(128)}, f32[96]{0:T(128)S(1)}, u32[]{:S(2)}) copy-start(f32[96]{0:T(128)S(1)} %fusion.115) | copy-start | bytes 1156
  150.6 88.6 %copy-start.53 = (bf16[96,256]{1,0:T(8,128)(2,1)}, bf16[96,256]{1,0:T(8,128)(2,1)S(1)}, u32[]{:S(2)}) copy-start(bf16[96,256]{1,0:T(8,128)(2,1)S(1)} %convolution_convert_fusion.4) | copy-start | bytes 147460
  151.7 80.2 %reduce-scatter.46.cloned.1.call-start = ((), (), s32[]{:S(2)}) async-start(), calls=%async_computation.25 | async-start | bytes 552960
  152.3 88.0 %copy-start.152 = (bf16[96,256]{1,0:T(8,128)(2,1)}, bf16[96,256]{1,0:T(8,128)(2,1)S(1)}, u32[]{:S(2)}) copy-start(bf16[96,256]{1,0:T(8,128)(2,1)S(1)} %convolution_convert_fusion.7) | copy-start | bytes 147460
  153.6 106.5 %all-gather.4.cloned.1.call-start = ((), (), s32[]{:S(2)}) async-start(), calls=%async_computation.15 | async-start | bytes 4644864 | tf_op jit(solution)/shard_map/all_gather | solution.py:296
  154.2 178.6 %all-gather.6.cloned.1.call-start = ((), (), s32[]{:S(2)}) async-start(), calls=%async_computation.16 | async-start | bytes 4644864 | tf_op jit(solution)/shard_map/all_gather | solution.py:297
  154.8 250.6 %all-gather.8.cloned.1.call-start = ((), (), s32[]{:S(2)}) async-start(), calls=%async_computation.17 | async-start | bytes 4644864 | tf_op jit(solution)/shard_map/all_gather | solution.py:298
  155.4 277.0 %reduce-scatter.52.cloned.1.call-start = ((), (), s32[]{:S(2)}) async-start(), calls=%async_computation.28 | async-start | bytes 552960
  239.6 97.4 %copy-start.135 = (f32[96]{0:T(128)}, f32[96]{0:T(128)S(1)}, u32[]{:S(2)}) copy-start(f32[96]{0:T(128)S(1)} %get-tuple-element.82) | copy-start | bytes 1156
  240.1 96.9 %copy-start.106 = (f32[96]{0:T(128)}, f32[96]{0:T(128)S(1)}, u32[]{:S(2)}) copy-start(f32[96]{0:T(128)S(1)} %fusion.124) | copy-start | bytes 1156
  240.1 96.9 %copy-start.107 = (f32[96]{0:T(128)}, f32[96]{0:T(128)S(1)}, u32[]{:S(2)}) copy-start(f32[96]{0:T(128)S(1)} %fusion.130) | copy-start | bytes 1156
  240.3 96.7 %copy-start.9 = (bf16[96,1152]{1,0:T(8,128)(2,1)}, bf16[96,1152]{1,0:T(8,128)(2,1)S(1)}, u32[]{:S(2)}) copy-start(bf16[96,1152]{1,0:T(8,128)(2,1)S(1)} %get-tuple-element.105) | copy-start | bytes 663556
  409.8 46.6 %reduce-scatter.48.cloned.1.call-start = ((), (), s32[]{:S(2)}) async-start(), calls=%async_computation.26 | async-start | bytes 552960
  418.2 80.1 %reduce-scatter.58.cloned.1.call-start = ((), (), s32[]{:S(2)}) async-start(), calls=%async_computation.31 | async-start | bytes 552960
  477.2 45.3 %reduce-scatter.54.cloned.1.call-start = ((), (), s32[]{:S(2)}) async-start(), calls=%async_computation.29 | async-start | bytes 552960
  487.1 114.1 %reduce-scatter.36.cloned.1.call-start = ((), (), s32[]{:S(2)}) async-start(), calls=%async_computation.20 | async-start | bytes 1327104 | tf_op jit(solution)/shard_map/reduce_scatter | solution.py:332
  539.2 128.7 %reduce-scatter.34.cloned.1.call-start = ((), (), s32[]{:S(2)}) async-start(), calls=%async_computation.19 | async-start | bytes 1327104 | tf_op jit(solution)/shard_map/reduce_scatter | solution.py:331
  543.5 148.6 %reduce-scatter.60.cloned.1.call-start = ((), (), s32[]{:S(2)}) async-start(), calls=%async_computation.32 | async-start | bytes 276480
  550.5 162.6 %reduce-scatter.56.cloned.1.call-start = ((), (), s32[]{:S(2)}) async-start(), calls=%async_computation.30 | async-start | bytes 276480
  553.9 225.3 %reduce-scatter.38.cloned.1.call-start = ((), (), s32[]{:S(2)}) async-start(), calls=%async_computation.21 | async-start | bytes 1327104 | tf_op jit(solution)/shard_map/reduce_scatter | solution.py:333
  557.7 288.6 %reduce-scatter.32.cloned.1.call-start = ((), (), s32[]{:S(2)}) async-start(), calls=%async_computation.18 | async-start | bytes 1327104 | tf_op jit(solution)/shard_map/reduce_scatter | solution.py:330
  559.7 108.3 %copy-start.23 = (bf16[192,1152]{1,0:T(8,128)(2,1)S(1)}, bf16[192,1152]{1,0:T(8,128)(2,1)}, u32[]{:S(2)}) copy-start(bf16[192,1152]{1,0:T(8,128)(2,1)} %param.18) | copy-start | bytes 1327108
  559.7 108.3 %copy-start.24 = (bf16[96,1728]{1,0:T(8,128)(2,1)S(1)}, bf16[96,1728]{1,0:T(8,128)(2,1)}, u32[]{:S(2)}) copy-start(bf16[96,1728]{1,0:T(8,128)(2,1)} %get-tuple-element.154) | copy-start | bytes 995332
  559.7 108.3 %copy-start.88 = (f32[96]{0:T(128)S(1)}, f32[96]{0:T(128)}, u32[]{:S(2)}) copy-start(f32[96]{0:T(128)} %copy-done.86) | copy-start | bytes 1156
  559.7 108.3 %copy-start.124 = (f32[96]{0:T(128)S(1)}, f32[96]{0:T(128)}, u32[]{:S(2)}) copy-start(f32[96]{0:T(128)} %fusion.131) | copy-start | bytes 1156
  559.8 108.3 %copy-start.133 = (f32[96]{0:T(128)S(1)}, f32[96]{0:T(128)}, u32[]{:S(2)}) copy-start(f32[96]{0:T(128)} %copy-done.132) | copy-start | bytes 1156
  559.8 286.6 %all-reduce.34.cloned.1.call-start = ((), (), s32[]{:S(2)}) async-start(), calls=%async_computation.33 | async-start | bytes 589824 | tf_op jit(solution)/shard_map/psum | solution.py:344
  667.9 327.7 %reduce-scatter.44.cloned.1.call-start = ((), (), s32[]{:S(2)}) async-start(), calls=%async_computation.24 | async-start | bytes 9289728 | tf_op jit(solution)/shard_map/reduce_scatter | solution.py:336
  676.0 468.1 %reduce-scatter.42.cloned.1.call-start = ((), (), s32[]{:S(2)}) async-start(), calls=%async_computation.23 | async-start | bytes 9289728 | tf_op jit(solution)/shard_map/reduce_scatter | solution.py:335
  682.8 609.9 %reduce-scatter.40.cloned.1.call-start = ((), (), s32[]{:S(2)}) async-start(), calls=%async_computation.22 | async-start | bytes 9289728 | tf_op jit(solution)/shard_map/reduce_scatter | solution.py:334
  (125 other events, 1990.1 us)
Sparse Core Ops, SparseCore 0:
  151.8 55.6 reduce-scatter.49
  210.6 21.1 reduce-scatter.45
  410.0 22.3 reduce-scatter.51
  435.3 21.0 reduce-scatter.47
  477.3 20.9 reduce-scatter.57
  501.3 21.1 reduce-scatter.53
  668.1 32.5 all-reduce.33
Sparse Core Ops, SparseCore 1:
  156.3 103.8 all-gather.3
  262.2 70.5 all-gather.5
  334.8 70.5 all-gather.7
  539.2 61.9 reduce-scatter.35
  604.6 63.2 reduce-scatter.33
  670.4 20.5 reduce-scatter.59
  693.5 19.5 reduce-scatter.55
  716.9 62.3 reduce-scatter.37
  783.1 63.2 reduce-scatter.31
  850.6 145.0 reduce-scatter.43
  999.8 144.3 reduce-scatter.41
  1148.5 144.3 reduce-scatter.39
where the time goes:
time: 1310 us; the launch traced here: 1300 us
  waiting for transfers between devices  933 us (71%)
  blocking collectives  221 us (17%)
  matrix products  85.1 us (6%)
  other arithmetic  21.7 us (2%)
  local copies, waits for them, and re-layouts  21.2 us (2%)
  between operations  20.9 us (2%)
    reduce_scatter x1, waiting for transfers between devices, on_device(): lax.psum_scatter(totals[6], 'dp', scatter_dimension=1, tiled=True)  149 us
    reduce_scatter x1, waiting for transfers between devices, on_device(): lax.psum_scatter(totals[4], 'dp', scatter_dimension=0, tiled=True)  149 us
    reduce_scatter x1, waiting for transfers between devices, on_device(): lax.psum_scatter(totals[5], 'dp', scatter_dimension=0, tiled=True)  148 us
    unnamed x27, waiting for transfers between devices  141 us
    all_gather x1, waiting for transfers between devices, on_device(): lax.all_gather(up_weight, 'dp', axis=0, tiled=True)  68.8 us
    all_gather x1, waiting for transfers between devices, on_device(): lax.all_gather(down_weight, 'dp', axis=1, tiled=True)  68.5 us
    reduce_scatter x1, waiting for transfers between devices, on_device(): lax.psum_scatter(totals[0], 'dp', scatter_dimension=0, tiled=True)  67.1 us
    reduce_scatter x1, waiting for transfers between devices, on_device(): lax.psum_scatter(totals[1], 'dp', scatter_dimension=0, tiled=True)  66.7 us
  transfers between devices with their start and end apart: 19, of which 17 were waited for; matrix products, arithmetic and copies ran while one was open for 6% of the time, Pallas kernels for 0%

commit v1 on v0

v1 whole, which is shorter than its diff:
```python
import jax
import jax.numpy as jnp
from jax import lax
from jax.sharding import PartitionSpec as P

WINDOW = 512


EPSILON = 1e-06
THETA_BASE = 10000.0
NEGATIVE = -1e30


def matmul(left_op, right_op):
    return jnp.dot(left_op, right_op, preferred_element_type=jnp.float32)


def inner_rows(left_op, right_op):
    return lax.dot_general(
        left_op, right_op, (((0,), (0,)), ((), ())), preferred_element_type=jnp.float32
    )


def inner_cols(left_op, right_op):
    return lax.dot_general(
        left_op, right_op, (((1,), (1,)), ((), ())), preferred_element_type=jnp.float32
    )


def normed(values, factor):
    return values * lax.rsqrt(jnp.mean(values * values, axis=-1, keepdims=True) + EPSILON) * factor


def rotate(values, cosine, sine_table):
    half_width = values.shape[-1] // 2
    leading = values[..., :half_width]
    trailing = values[..., half_width:]
    return jnp.concatenate(
        [leading * cosine - trailing * sine_table, trailing * cosine + leading * sine_table],
        axis=-1,
    )


def layout(lengths, row_count):
    batches, docs = lengths.shape
    total = batches * row_count
    index = jnp.arange(total, dtype=jnp.int32)
    buffer = index // row_count
    inside = index % row_count
    order = jnp.arange(docs, dtype=jnp.int32)
    ends = jnp.sum(
        jnp.where(order[None, :, None] >= order[None, None, :], lengths[:, None, :], 0), axis=2
    )
    row_ends = jnp.repeat(ends, row_count, axis=0)
    row_lengths = jnp.repeat(lengths, row_count, axis=0)
    passed = inside[:, None] >= row_ends
    segment = jnp.sum(passed.astype(jnp.int32), axis=1)
    begins = jnp.sum(jnp.where(passed, row_lengths, 0), axis=1)
    position = inside - begins
    live_rows = (segment < docs).astype(jnp.float32)
    group = buffer * (docs + 1) + segment
    allowed = (
        (group[:, None] == group[None, :])
        & (index[None, :] <= index[:, None])
        & (index[:, None] - index[None, :] < WINDOW)
    )
    return (position, live_rows, allowed)


def angles(position, head_width):
    half_width = head_width // 2
    frequency = THETA_BASE ** (-2.0 * jnp.arange(half_width, dtype=jnp.float32) / head_width)
    turned = position.astype(jnp.float32)[:, None] * frequency[None, :]
    return (jnp.cos(turned), jnp.sin(turned))


def on_device(
    tokens,
    doc_lengths,
    cotangent,
    query_weight,
    key_weight,
    value_weight,
    out_weight,
    gate_weight,
    up_weight,
    down_weight,
    pre_attn_gain,
    post_attn_gain,
    pre_ffn_gain,
    post_ffn_gain,
    query_gain,
    key_gain,
):
    low = jnp.bfloat16
    full = jnp.float32
    dp = lax.axis_size("dp")
    mp = lax.axis_size("mp")
    shard = lax.axis_index("mp")
    rows, width = tokens.shape
    share = width // dp
    head_width = query_weight.shape[1]
    units = gate_weight.shape[1] // dp
    own_rows = rows // mp
    own = (shard * own_rows, own_rows)

    gain_head = query_gain.shape[0]
    gains = jnp.concatenate(
        [pre_attn_gain, post_attn_gain, pre_ffn_gain, post_ffn_gain, query_gain, key_gain]
    )
    block = jnp.concatenate([query_weight, key_weight, value_weight, out_weight.T], axis=1)
    gains_row = jnp.pad(gains, (0, block.shape[1] - gains.shape[0]))[None]
    packed = jnp.concatenate([block, jnp.pad(gains_row, ((0, 15), (0, 0)))], axis=0)
    packed = lax.all_gather(packed, "dp", axis=0, tiled=False)
    attn_w = packed[:, :share].reshape(width, 4 * head_width)
    qkv_w = attn_w[:, : 3 * head_width]
    out_wt = attn_w[:, 3 * head_width :]
    all_gains = packed[:, share].astype(full)
    gain_one, gain_two, gain_three, gain_four = (
        all_gains[:, i * share : (i + 1) * share].reshape(width) for i in range(4)
    )
    query_g = all_gains[:, 4 * share : 4 * share + gain_head].reshape(head_width)
    key_g = all_gains[:, 4 * share + gain_head : 4 * share + 2 * gain_head].reshape(head_width)

    ffn_block = jnp.stack([gate_weight, up_weight, down_weight.T], axis=0)
    ffn_block = ffn_block.reshape(3, share, dp, units).transpose(2, 1, 0, 3)
    ffn_block = ffn_block.reshape(dp, share, 3 * units)
    ffn_w = lax.all_to_all(ffn_block, "dp", split_axis=0, concat_axis=0, tiled=True)
    ffn_w = ffn_w.reshape(width, 3 * units)
    glu_w = ffn_w[:, : 2 * units]
    down_wt = ffn_w[:, 2 * units :]

    inputs = tokens.astype(full)
    position, live_rows, allowed = layout(doc_lengths, rows // doc_lengths.shape[0])
    cosine, sine_table = angles(position, head_width)
    normed_in = normed(inputs, gain_one).astype(low)
    projected = matmul(normed_in, qkv_w)
    query_pre = projected[:, :head_width]
    key_pre = projected[:, head_width : 2 * head_width]
    value_low = projected[:, 2 * head_width :].astype(low)
    query_low = rotate(normed(query_pre, query_g), cosine, sine_table).astype(low)
    key_low = rotate(normed(key_pre, key_g), cosine, sine_table).astype(low)
    score_scale = head_width ** (-0.5)
    scores = inner_cols(query_low, key_low) * score_scale
    scores = jnp.where(allowed, scores, NEGATIVE)
    row_peak = jnp.max(scores, axis=1, keepdims=True)
    raised = jnp.exp(scores - row_peak)
    attention = raised / jnp.sum(raised, axis=1, keepdims=True)
    attention_low = attention.astype(low)
    attended = matmul(attention_low, value_low).astype(low)
    attn_part = inner_cols(attended, out_wt).astype(low)
    attn_sum = lax.psum_scatter(attn_part, "mp", scatter_dimension=0, tiled=True).astype(full)

    inputs_own = lax.dynamic_slice_in_dim(tokens, *own, axis=0).astype(full)
    upstream = lax.dynamic_slice_in_dim(cotangent, *own, axis=0).astype(full)
    live = lax.dynamic_slice_in_dim(live_rows, *own, axis=0)[:, None]

    def post_norm(values, factor):
        return normed(values, factor) * live

    attn_out, back_two = jax.vjp(post_norm, attn_sum, gain_two)
    middle = inputs_own + attn_out
    normed_mid_own, back_three = jax.vjp(normed, middle, gain_three)
    normed_mid = lax.all_gather(normed_mid_own.astype(low), ("dp", "mp"), axis=0, tiled=True)
    glu_pre = matmul(normed_mid, glu_w)
    gate_proj = glu_pre[:, :units]
    up_proj = glu_pre[:, units:]

    def glu(gate_in, up_in):
        return jax.nn.gelu(gate_in, approximate=True) * up_in

    hidden_full, back_glu = jax.vjp(glu, gate_proj, up_proj)
    hidden = hidden_full.astype(low)
    ffn_part = inner_cols(hidden, down_wt).astype(low)
    ffn_sum = lax.psum_scatter(ffn_part, ("dp", "mp"), scatter_dimension=0, tiled=True).astype(full)
    ffn_out, back_four = jax.vjp(post_norm, ffn_sum, gain_four)
    mixed_own = (middle + ffn_out).astype(low)

    d_ffn_own, grad_four = back_four(upstream)
    d_ffn = lax.all_gather(d_ffn_own.astype(low), ("dp", "mp"), axis=0, tiled=True)
    grad_down_t = inner_rows(d_ffn, hidden)
    d_hidden = matmul(d_ffn, down_wt)
    d_gate, d_up = back_glu(d_hidden)
    d_glu = jnp.concatenate([d_gate.astype(low), d_up.astype(low)], axis=1)
    d_mid_part = inner_cols(d_glu, glu_w).astype(low)
    d_mid = lax.psum_scatter(d_mid_part, ("dp", "mp"), scatter_dimension=0, tiled=True).astype(full)
    grad_glu = inner_rows(normed_mid, d_glu)
    ffn_grad = jnp.concatenate([grad_glu, grad_down_t], axis=1).astype(low)
    ffn_grad = ffn_grad.reshape(dp, share, 3 * units)
    ffn_grad = lax.all_to_all(ffn_grad, "dp", split_axis=0, concat_axis=0, tiled=True)
    ffn_grad = ffn_grad.reshape(dp, share, 3, units).transpose(2, 1, 0, 3)
    ffn_grad = ffn_grad.reshape(3, share, dp * units).astype(full)

    d_mid_add, grad_three = back_three(d_mid)
    d_middle = upstream + d_mid_add
    d_attn_own, grad_two = back_two(d_middle)
    d_attn = lax.all_gather(d_attn_own.astype(low), "mp", axis=0, tiled=True)

    grad_out_t = inner_rows(d_attn, attended)
    d_attended = matmul(d_attn, out_wt).astype(low)
    d_value = inner_rows(attention_low, d_attended).astype(low)
    d_probs = inner_cols(d_attended, value_low)
    d_scores = attention * (d_probs - jnp.sum(attention * d_probs, axis=1, keepdims=True))
    d_scores = d_scores.astype(low)
    d_query_rot = matmul(d_scores, key_low) * score_scale
    d_key_rot = inner_rows(d_scores, query_low) * score_scale

    def turned(values, factor):
        return rotate(normed(values, factor), cosine, sine_table)

    _, back_query = jax.vjp(turned, query_pre, query_g)
    d_query_pre, grad_qgain = back_query(d_query_rot)
    _, back_key = jax.vjp(turned, key_pre, key_g)
    d_key_pre, grad_kgain = back_key(d_key_rot)
    d_qkv = jnp.concatenate([d_query_pre.astype(low), d_key_pre.astype(low), d_value], axis=1)
    d_in_part = inner_cols(d_qkv, qkv_w).astype(low)
    d_in = lax.psum_scatter(d_in_part, "mp", scatter_dimension=0, tiled=True).astype(full)
    grad_qkv = inner_rows(normed_in, d_qkv)
    _, back_one = jax.vjp(normed, inputs_own, gain_one)
    d_in_add, grad_one = back_one(d_in)
    tokens_grad_own = d_middle + d_in_add

    pieces = [g.reshape(dp, -1) for g in (grad_one, grad_two, grad_three, grad_four, grad_qgain, grad_kgain)]
    gains_grad = jnp.concatenate(pieces, axis=1)
    gains_grad = jnp.pad(gains_grad, ((0, 0), (0, 4 * head_width - gains_grad.shape[1])))
    weights_grad = jnp.concatenate([grad_qkv, grad_out_t], axis=1).reshape(dp, share, 4 * head_width)
    owned = jnp.concatenate(
        [weights_grad, jnp.pad(gains_grad[:, None], ((0, 0), (0, 15), (0, 0)))], axis=1
    ).astype(low)
    owned = lax.psum_scatter(owned, "dp", scatter_dimension=0, tiled=True)[0].astype(full)
    shared = jnp.concatenate(
        [
            owned[:share, head_width : 3 * head_width].reshape(-1),
            owned[share, : 4 * share + 2 * gain_head],
        ]
    )
    shared = lax.psum(shared, "mp")
    kv_grad = shared[: 2 * share * head_width].reshape(share, 2 * head_width)
    gain_out = shared[2 * share * head_width :]
    mixed = lax.all_gather(mixed_own, "mp", axis=0, tiled=True)
    tokens_grad = lax.all_gather(tokens_grad_own.astype(low), "mp", axis=0, tiled=True).astype(full)
    return (
        mixed,
        tokens_grad,
        owned[:share, :head_width],
        kv_grad[:, :head_width],
        kv_grad[:, head_width:],
        owned[:share, 3 * head_width :].T,
        ffn_grad[0],
        ffn_grad[1],
        ffn_grad[2].T,
        gain_out[:share],
        gain_out[share : 2 * share],
        gain_out[2 * share : 3 * share],
        gain_out[3 * share : 4 * share],
        gain_out[4 * share : 4 * share + gain_head],
        gain_out[4 * share + gain_head :],
    )


def solution(mesh):
    placed = (
        P("dp", None),
        P("dp", None),
        P("dp", None),
        P("dp", "mp"),
        P("dp", None),
        P("dp", None),
        P("mp", "dp"),
        P("dp", "mp"),
        P("dp", "mp"),
        P("mp", "dp"),
        P("dp"),
        P("dp"),
        P("dp"),
        P("dp"),
        P("dp"),
        P("dp"),
    )
    return jax.shard_map(
        on_device,
        mesh=mesh,
        in_specs=placed,
        out_specs=(
            P("dp", None),
            P("dp", None),
            P("dp", "mp"),
            P("dp", None),
            P("dp", None),
            P("mp", "dp"),
            P("dp", "mp"),
            P("dp", "mp"),
            P("mp", "dp"),
            P("dp"),
            P("dp"),
            P("dp"),
            P("dp"),
            P("dp"),
            P("dp"),
        ),
        check_vma=False,
    )
```

time: 1310 us -> 654 us (0.50)
  waiting for transfers between devices: 933 us -> 378 us
  blocking collectives: 221 us -> 140 us
  matrix products: 85.1 us -> 31.7 us
  local copies, waits for them, and re-layouts: 21.2 us -> 54 us
    reduce_scatter x7 -> x5, waiting for transfers between devices: 635 us -> 235 us  [the longest x1 102 us: on_device(): lax.psum_scatter(ffn_part, ('dp', 'mp'), scatter_dimension=0, tiled=True)]
    unnamed x27 -> x9, waiting for transfers between devices: 141 us -> 0.15 us
    all_gather x12 -> x3, blocking collectives: 161 us -> 23.2 us  [the longest x1 8.91 us: on_device(): d_attn = lax.all_gather(d_attn_own.astype(low), 'mp', axis=0, tiled=True)]
    all_to_all x0 -> x2, blocking collectives: none -> 117 us  [the longest x1 59.2 us: on_device(): lax.all_to_all(ffn_grad, 'dp', split_axis=0, concat_axis=0, tiled=True)]
    unnamed x2 -> x0, blocking collectives: 47.8 us -> none
    all_gather x3, waiting for transfers between devices: 157 us -> 112 us  [the longest x1 60.8 us: on_device(): lax.all_gather(d_ffn_own.astype(low), ('dp', 'mp'), axis=0, tiled=True)]
    psum x1, waiting for transfers between devices: 0.01 us -> 30.8 us  [on_device(): shared = lax.psum(shared, 'mp')]
    dot_general x18 -> x6, matrix products: 35 us -> 10.7 us  [inner_rows(): lax.dot_general(left_op, right_op, (((0,), (0,)), ((), ())), preferred_el...]
  transfers between devices with their start and end apart: 19 -> 9, of which waited for: 17 -> 7; matrix products, arithmetic and copies ran while one was open for 6% -> 9% of each run, Pallas kernels for 0% -> 0%
where the time goes in v1:
time: 654 us; the launch traced here: 651 us
  waiting for transfers between devices  378 us (58%)
  blocking collectives  140 us (21%)
  local copies, waits for them, and re-layouts  54 us (8%)
  other arithmetic  32.3 us (5%)
  matrix products  31.7 us (5%)
  between operations  15.1 us (2%)
    reduce_scatter x1, waiting for transfers between devices, on_device(): lax.psum_scatter(ffn_part, ('dp', 'mp'), scatter_dimension=0, tiled=True)  102 us
    reduce_scatter x1, waiting for transfers between devices, on_device(): lax.psum_scatter(d_mid_part, ('dp', 'mp'), scatter_dimension=0, tiled=True)  100 us
    all_gather x1, waiting for transfers between devices, on_device(): lax.all_gather(d_ffn_own.astype(low), ('dp', 'mp'), axis=0, tiled=True)  60.8 us
    all_to_all x1, blocking collectives, on_device(): lax.all_to_all(ffn_grad, 'dp', split_axis=0, concat_axis=0, tiled=True)  59.2 us
    all_to_all x1, blocking collectives, on_device(): lax.all_to_all(ffn_block, 'dp', split_axis=0, concat_axis=0, tiled=True)  57.9 us
    all_gather x1, waiting for transfers between devices, on_device(): packed = lax.all_gather(packed, 'dp', axis=0, tiled=False)  50.8 us
    psum x1, waiting for transfers between devices, on_device(): shared = lax.psum(shared, 'mp')  30.8 us
    reduce_scatter x1, waiting for transfers between devices, on_device(): lax.psum_scatter(attn_part, 'mp', scatter_dimension=0, tiled=True)  21.6 us
  transfers between devices with their start and end apart: 9, of which 7 were waited for; matrix products, arithmetic and copies ran while one was open for 9% of the time, Pallas kernels for 0%

profile of v1, /device:TPU:13, one launch (start us, length us, event | category | flops | bytes accessed | tf_op | source)
XLA Modules:
  0.0 651.5 jit_solution(11283578642979378089)
XLA Ops:
  7.2 4.1 concatenate.49
  11.3 1.8 fusion.25
  15.0 1.2 fusion.16
  16.2 50.8 %all-gather.9.cloned.1.call-done = bf16[1280,1024]{1,0:T(8,128)(2,1)} async-done(((bf16[160,1024]{1,0:T(8,128)(2,1)}), bf16[1280,1024]{1,0:T(8,128)(2,1)}) %all-gather.9.cloned.1.call-update) | async-done | bytes 2621456 | tf_op jit(solution)/shard_map/all_gather | solution.py:114
  67.9 2.1 slice.161
  74.9 1.1 convolution_convert_fusion.6
  76.4 21.6 %reduce-scatter.6.cloned.1.call-done = bf16[48,1152]{1,0:T(8,128)(2,1)} async-done(((bf16[192,1152]{1,0:T(8,128)(2,1)}), bf16[48,1152]{1,0:T(8,128)(2,1)}) %reduce-scatter.6.cloned.1.call-update) | async-done | bytes 110608 | tf_op jit(solution)/shard_map/reduce_scatter | solution.py:152
  99.5 1.2 multiply_reduce_fusion
  100.8 1.7 multiply_convert_fusion.2
  105.4 1.9 copy.61
  109.6 4.4 maximum_bitcast_fusion
  114.0 3.1 reshape.329
  117.2 57.9 %all_to_all.10 = bf16[8,144,648]{2,1,0:T(8,128)(2,1)S(1)} all-to-all(bf16[8,144,648]{2,1,0:T(8,128)(2,1)} %reshape.329), channel_id=1, replica_groups=mesh['dp'=8,'mp'=4] {'dp'}, dimensions={0} | all-to-all | bytes 2985984 | tf_op jit(solution)/shard_map/all_to_all | solution.py:128
  175.1 4.0 fusion.14
  179.0 1.5 copy-done.7
  181.0 3.3 convolution_convert_fusion
  185.1 101.8 %reduce-scatter.8.cloned.1.call-done = bf16[48,1152]{1,0:T(8,128)(2,1)} async-done(((bf16[1536,1152]{1,0:T(8,128)(2,1)}), bf16[48,1152]{1,0:T(8,128)(2,1)}) %reduce-scatter.8.cloned.1.call-update) | async-done | bytes 110608 | tf_op jit(solution)/shard_map/reduce_scatter | solution.py:175
  288.0 1.2 fusion.41
  289.2 1.7 fusion.44
  290.9 60.8 %all-gather.7.cloned.1.call-done = bf16[1536,1152]{1,0:T(8,128)(2,1)} async-done(((bf16[48,1152]{1,0:T(8,128)(2,1)}), bf16[1536,1152]{1,0:T(8,128)(2,1)}) %all-gather.7.cloned.1.call-update) | async-done | bytes 3538960 | tf_op jit(solution)/shard_map/all_gather | solution.py:180
  351.8 5.0 fusion.11
  357.6 4.2 convolution_convert_fusion.1
  362.1 100.1 %reduce-scatter.10.cloned.1.call-done = bf16[48,1152]{1,0:T(8,128)(2,1)} async-done(((bf16[1536,1152]{1,0:T(8,128)(2,1)}), bf16[48,1152]{1,0:T(8,128)(2,1)}) %reduce-scatter.10.cloned.1.call-update) | async-done | bytes 110608 | tf_op jit(solution)/shard_map/reduce_scatter | solution.py:186
  462.1 1.2 fusion.42
  463.4 2.0 fusion.39
  465.6 8.9 %all_gather.26 = bf16[192,1152]{1,0:T(8,128)(2,1)S(1)} all-gather(bf16[48,1152]{1,0:T(8,128)(2,1)S(1)} %fusion.45), channel_id=1, replica_groups=mesh['dp'=8,'mp'=4] {'mp'}, dimensions={0}, use_global_device_ids=true | all-gather | bytes 552960 | tf_op jit(solution)/shard_map/all_gather | solution.py:197
  477.0 1.5 convolution_convert_fusion.7
  478.8 1.4 convolution_convert_fusion.4
  480.6 1.8 convolution_convert_fusion.2
  482.4 1.7 pad_maximum_fusion
  484.0 2.9 copy.63
  486.9 11.5 %reduce-scatter.12.cloned.1.call-done = bf16[48,1152]{1,0:T(8,128)(2,1)} async-done(((bf16[192,1152]{1,0:T(8,128)(2,1)}), bf16[48,1152]{1,0:T(8,128)(2,1)}) %reduce-scatter.12.cloned.1.call-update) | async-done | bytes 110608 | tf_op jit(solution)/shard_map/reduce_scatter | solution.py:217
  498.5 1.2 fusion.43
  499.9 1.8 fusion.1
  501.8 3.1 convolution_convert_fusion.5
  505.1 4.1 convolution_convert_fusion.3
  510.5 59.2 %all_to_all.11 = bf16[8,144,648]{2,1,0:T(8,128)(2,1)S(1)} all-to-all(bf16[8,144,648]{2,1,0:T(8,128)(2,1)S(1)} %pad_maximum_fusion.1), channel_id=1, replica_groups=mesh['dp'=8,'mp'=4] {'dp'}, dimensions={0} | all-to-all | bytes 2985984 | tf_op jit(solution)/shard_map/all_to_all | solution.py:190
  569.7 4.9 reshape.342
  574.6 8.8 %fusion.116 = (f32[1,144,8,216]{3,0,1,2:T(1,128)S(1)}, f32[1,144,8,216]{3,0,1,2:T(1,128)S(1)}, f32[1,144,8,216]{3,0,1,2:T(1,128)S(1)}) fusion(f32[3,144,8,216]{3,0,1,2:T(4,128)} %bitcast.45), kind=kLoop, calls=%fused_computation.220 | loop fusion | bytes 5971968 | tf_op jit(solution)/shard_map/slice | solution.py:251
  584.1 1.4 squeeze.17
  586.2 1.4 squeeze.16
  588.4 1.4 squeeze.15
  589.8 7.4 %all_gather.24 = bf16[192,1152]{1,0:T(8,128)(2,1)S(1)} all-gather(bf16[48,1152]{1,0:T(8,128)(2,1)S(1)} %copy-done.18), channel_id=1, replica_groups=mesh['dp'=8,'mp'=4] {'mp'}, dimensions={0}, use_global_device_ids=true | all-gather | bytes 552960 | tf_op jit(solution)/shard_map/all_gather | solution.py:240
  598.3 6.8 %all_gather.27 = bf16[192,1152]{1,0:T(8,128)(2,1)S(1)} all-gather(bf16[48,1152]{1,0:T(8,128)(2,1)S(1)} %fusion.47), channel_id=1, replica_groups=mesh['dp'=8,'mp'=4] {'mp'}, dimensions={0}, use_global_device_ids=true | all-gather | bytes 552960 | tf_op jit(solution)/shard_map/all_gather | solution.py:241
  606.1 1.0 bitcast_convert_fusion
  608.8 30.8 %all-reduce.10.cloned.1.call-done = f32[74368]{0:T(1024)} async-done(((f32[74368]{0:T(1024)}), f32[74368]{0:T(1024)}) %all-reduce.10.cloned.1.call-update) | async-done | bytes 297488 | tf_op jit(solution)/shard_map/psum | solution.py:237
  641.4 1.3 fusion.117
  642.7 1.5 fusion.118
  (247 shorter events, 30.7 us)
Async XLA Ops:
  7.2 59.8 %all-gather.9.cloned.1.call-start = ((), (), s32[]{:S(2)}) async-start(), calls=%async_computation.15 | async-start | bytes 2949120 | tf_op jit(solution)/shard_map/all_gather | solution.py:114
  13.1 84.8 %reduce-scatter.6.cloned.1.call-start = ((), (), s32[]{:S(2)}) async-start(), calls=%async_computation.7 | async-start | bytes 552960 | tf_op jit(solution)/shard_map/reduce_scatter | solution.py:152
  15.0 57.3 %copy-start.57 = (f32[128]{0:T(128)}, f32[128]{0:T(128)S(1)}, u32[]{:S(2)}) copy-start(f32[128]{0:T(128)S(1)} %multiply_power_fusion) | copy-start | bytes 1540
  16.2 55.0 %copy-start.59 = (f32[192]{0:T(256)}, f32[192]{0:T(256)S(1)}, u32[]{:S(2)}) copy-start(f32[192]{0:T(256)S(1)} %add_rsqrt_fusion) | copy-start | bytes 2308
  16.2 56.1 %copy-start.45 = (f32[192]{0:T(256)}, f32[192]{0:T(256)S(1)}, u32[]{:S(2)}) copy-start(f32[192]{0:T(256)S(1)} %fusion.98) | copy-start | bytes 2308
  67.9 3.3 copy-start.6
  70.0 3.9 copy-start.4
  71.8 2.1 copy-start.1
  73.3 29.2 %copy-start.14 = (bf16[144,1728]{1,0:T(8,128)(2,1)S(1)}, bf16[144,1728]{1,0:T(8,128)(2,1)}, u32[]{:S(2)}) copy-start(bf16[144,1728]{1,0:T(8,128)(2,1)} %param.23) | copy-start | bytes 1492996
  76.0 99.0 %all-gather.5.cloned.1.call-start = ((), (), s32[]{:S(2)}) async-start(), calls=%async_computation.8 | async-start | bytes 3649536 | tf_op jit(solution)/shard_map/all_gather | solution.py:164
  76.2 27.3 %copy-start.33 = (f32[48]{0:T(128)}, f32[48]{0:T(128)S(1)}, u32[]{:S(2)}) copy-start(f32[48]{0:T(128)S(1)} %dynamic_slice.10) | copy-start | bytes 580
  99.5 4.0 copy-start.43
  99.5 4.9 copy-start.15
  100.7 2.8 copy-start.65
  100.7 2.8 copy-start.51
  102.5 184.5 %reduce-scatter.8.cloned.1.call-start = ((), (), s32[]{:S(2)}) async-start(), calls=%async_computation.9 | async-start | bytes 3649536 | tf_op jit(solution)/shard_map/reduce_scatter | solution.py:175
  104.5 2.9 copy-start.16
  179.0 1.5 copy-start.7
  184.4 103.6 %copy-start.21 = (bf16[192,1152]{1,0:T(8,128)(2,1)S(1)}, bf16[192,1152]{1,0:T(8,128)(2,1)}, u32[]{:S(2)}) copy-start(bf16[192,1152]{1,0:T(8,128)(2,1)} %param.18) | copy-start | bytes 1327108
  184.4 103.6 %copy-start.34 = (f32[48]{0:T(128)S(1)}, f32[48]{0:T(128)}, u32[]{:S(2)}) copy-start(f32[48]{0:T(128)} %copy-done.33) | copy-start | bytes 580
  184.4 167.4 %all-gather.7.cloned.1.call-start = ((), (), s32[]{:S(2)}) async-start(), calls=%async_computation.10 | async-start | bytes 3649536 | tf_op jit(solution)/shard_map/all_gather | solution.py:180
  290.9 171.3 %reduce-scatter.10.cloned.1.call-start = ((), (), s32[]{:S(2)}) async-start(), calls=%async_computation.11 | async-start | bytes 3649536 | tf_op jit(solution)/shard_map/reduce_scatter | solution.py:186
  356.8 5.0 copy-start.68
  361.8 100.3 %copy-start.3 = (bf16[48,1152]{1,0:T(8,128)(2,1)S(1)}, bf16[48,1152]{1,0:T(8,128)(2,1)}, u32[]{:S(2)}) copy-start(bf16[48,1152]{1,0:T(8,128)(2,1)} %reduce-scatter.6.cloned.1.call-done) | copy-start | bytes 331780
  361.8 100.3 %copy-start.44 = (f32[48]{0:T(128)S(1)}, f32[48]{0:T(128)}, u32[]{:S(2)}) copy-start(f32[48]{0:T(128)} %copy-done.43) | copy-start | bytes 580
  361.8 100.3 %copy-start.52 = (f32[48]{0:T(128)S(1)}, f32[48]{0:T(128)}, u32[]{:S(2)}) copy-start(f32[48]{0:T(128)} %copy-done.51) | copy-start | bytes 580
  361.8 101.6 %copy-start.66 = (f32[48]{0:T(128)S(1)}, f32[48]{0:T(128)}, u32[]{:S(2)}) copy-start(f32[48]{0:T(128)} %copy-done.65) | copy-start | bytes 580
  361.8 101.6 %copy-start.11 = (bf16[48,1152]{1,0:T(8,128)(2,1)S(1)}, bf16[48,1152]{1,0:T(8,128)(2,1)}, u32[]{:S(2)}) copy-start(bf16[48,1152]{1,0:T(8,128)(2,1)} %reduce-scatter.8.cloned.1.call-done) | copy-start | bytes 331780
  361.9 103.6 %copy-start.64 = (f32[48]{0:T(128)S(1)}, f32[48]{0:T(128)}, u32[]{:S(2)}) copy-start(f32[48]{0:T(128)} %copy-done.63) | copy-start | bytes 580
  361.9 112.7 %copy-start.5 = (bf16[8,144,1024]{2,1,0:T(8,128)(2,1)S(1)}, bf16[8,144,1024]{2,1,0:T(8,128)(2,1)}, u32[]{:S(2)}) copy-start(bf16[8,144,1024]{2,1,0:T(8,128)(2,1)} %copy-done.4) | copy-start | bytes 7077892
  361.9 136.6 %reduce-scatter.12.cloned.1.call-start = ((), (), s32[]{:S(2)}) async-start(), calls=%async_computation.12 | async-start | bytes 552960 | tf_op jit(solution)/shard_map/reduce_scatter | solution.py:217
  362.0 112.9 %copy-start.13 = (f32[192,192]{0,1:T(8,128)S(1)}, f32[192,192]{0,1:T(8,128)}, u32[]{:S(2)}) copy-start(f32[192,192]{0,1:T(8,128)} %copy-done.12) | copy-start | bytes 442372
  362.1 112.9 %copy-start.54 = (f32[192]{0:T(256)S(1)}, f32[192]{0:T(256)}, u32[]{:S(2)}) copy-start(f32[192]{0:T(256)} %copy-done.53) | copy-start | bytes 2308
  362.1 112.9 %copy-start.56 = (f32[192]{0:T(256)S(1)}, f32[192]{0:T(256)}, u32[]{:S(2)}) copy-start(f32[192]{0:T(256)} %copy-done.55) | copy-start | bytes 2308
  463.4 23.5 %copy-start.61 = (f32[48]{0:T(128)}, f32[48]{0:T(128)S(1)}, u32[]{:S(2)}) copy-start(f32[48]{0:T(128)S(1)} %get-tuple-element.29) | copy-start | bytes 580
  465.5 10.0 %copy-start.8 = (f32[48,1152]{1,0:T(8,128)}, f32[48,1152]{1,0:T(8,128)S(1)}, u32[]{:S(2)}) copy-start(f32[48,1152]{1,0:T(8,128)S(1)} %get-tuple-element.34) | copy-start | bytes 663556
  465.5 9.7 %copy-start.2 = (f32[192,768]{1,0:T(8,128)S(1)}, f32[192,768]{1,0:T(8,128)}, u32[]{:S(2)}) copy-start(f32[192,768]{1,0:T(8,128)} %copy-done.1) | copy-start | bytes 1769476
  475.2 1.8 copy-start.67
  477.0 1.8 copy-start.20
  477.0 3.6 copy-start.31
  477.0 3.6 copy-start.60
  478.5 127.6 %reduce-scatter.14.cloned.1.call-start = ((), (), s32[]{:S(2)}) async-start(), calls=%async_computation.13 | async-start | bytes 2949120 | tf_op jit(solution)/shard_map/reduce_scatter | solution.py:230
  501.7 3.4 copy-start.69
  501.7 137.9 %all-reduce.10.cloned.1.call-start = ((), (), s32[]{:S(2)}) async-start(), calls=%async_computation.14 | async-start | bytes 598016 | tf_op jit(solution)/shard_map/psum | solution.py:237
  587.6 2.2 copy-start.18
  588.3 8.9 %copy-start.62 = (f32[48]{0:T(128)S(1)}, f32[48]{0:T(128)}, u32[]{:S(2)}) copy-start(f32[48]{0:T(128)} %copy-done.61) | copy-start | bytes 580
  588.3 8.9 %copy-start.9 = (f32[48,1152]{1,0:T(8,128)S(1)}, f32[48,1152]{1,0:T(8,128)}, u32[]{:S(2)}) copy-start(f32[48,1152]{1,0:T(8,128)} %copy-done.8) | copy-start | bytes 663556
  588.4 8.9 %copy-start.17 = (bf16[48,1152]{1,0:T(8,128)(2,1)S(1)}, bf16[48,1152]{1,0:T(8,128)(2,1)}, u32[]{:S(2)}) copy-start(bf16[48,1152]{1,0:T(8,128)(2,1)} %reduce-scatter.12.cloned.1.call-done) | copy-start | bytes 331780
  (32 other events, 31.8 us)
Sparse Core Ops, SparseCore 0:
  13.2 53.6 all-gather.8
  76.2 21.7 reduce-scatter.5
  102.6 69.2 all-gather.4
  184.5 102.3 reduce-scatter.7
  291.0 60.7 all-gather.6
  362.0 100.0 reduce-scatter.9
  478.6 19.7 reduce-scatter.11
  502.0 91.5 reduce-scatter.13
  608.1 31.4 all-reduce.9

commit v2 on v1

--- a/solution.py
+++ b/solution.py
@@ -1,6 +1,11 @@
+import functools
+import math
+
 import jax
 import jax.numpy as jnp
 from jax import lax
+from jax.experimental import pallas as pl
+from jax.experimental.pallas import tpu as pltpu
 from jax.sharding import PartitionSpec as P
 
 WINDOW = 512
@@ -72,6 +77,273 @@
     frequency = THETA_BASE ** (-2.0 * jnp.arange(half_width, dtype=jnp.float32) / head_width)
     turned = position.astype(jnp.float32)[:, None] * frequency[None, :]
     return (jnp.cos(turned), jnp.sin(turned))
+
+
+MESH = pl.DeviceIdType.MESH
+
+
+def axis_factors(axes):
+    dims = []
+    for axis in axes:
+        left = lax.axis_size(axis)
+        while left > 1:
+            size = 4 if axis == "dp" and left >= 8 else 2
+            left //= size
+            dims.append((axis, size, left))
+    return dims
+
+
+def chunk_orders(dims, width):
+    order = list(reversed(range(len(dims))))
+    lanes = width // 128
+    if dims[0][0] != "dp" or width % 128 or lanes < 2:
+        return [(0, width, order)]
+    swapped = list(order)
+    at = 1 if len(dims) >= 3 else 0
+    swapped[at], swapped[at + 1] = swapped[at + 1], swapped[at]
+    half = (lanes + 1) // 2 * 128
+    return [(0, half, order), (half, width - half, swapped)]
+
+
+def places(dims):
+    return [lax.rem(lax.axis_index(axis) // stride, size) for axis, size, stride in dims]
+
+
+def peer(dims, coords, which, step):
+    axis, size, stride = dims[which]
+    target = lax.rem(coords[which] + step, size)
+    device = {name: lax.axis_index(name) for name in ("dp", "mp")}
+    device[axis] = device[axis] + (target - coords[which]) * stride
+    return target, (device["dp"], device["mp"])
+
+
+def greet(dims, coords):
+    barrier = pltpu.get_barrier_semaphore()
+    count = 0
+    for which, (_, size, _) in enumerate(dims):
+        for step in range(1, size):
+            _, device = peer(dims, coords, which, step)
+            pl.semaphore_signal(barrier, inc=1, device_id=device, device_id_type=MESH)
+            count += 1
+    pl.semaphore_wait(barrier, count)
+
+
+def slots_of(dims):
+    firsts, total = [], 0
+    for _, size, _ in dims:
+        firsts.append(total)
+        total += size - 1
+    return firsts, total
+
+
+def gather_kernel(dims, chunks, firsts, x_ref, o_ref, send_sem, recv_sem):
+    coords = places(dims)
+    o_ref[tuple(coords)] = x_ref[...]
+    greet(dims, coords)
+
+    def begin(k, stage):
+        first, columns, order = chunks[k]
+        order = order[::-1]
+        done = order[:stage]
+        which = order[stage]
+        index = tuple(
+            pl.ds(0, dims[i][1]) if i in done else coords[i] for i in range(len(dims))
+        )
+        block = o_ref.at[index + (slice(None), pl.ds(first, columns))]
+        copies = []
+        for step in range(1, dims[which][1]):
+            slot = firsts[which] + step - 1
+            _, device = peer(dims, coords, which, step)
+            copy = pltpu.make_async_remote_copy(
+                src_ref=block,
+                dst_ref=block,
+                send_sem=send_sem.at[k, slot],
+                recv_sem=recv_sem.at[k, slot],
+                device_id=device,
+                device_id_type=MESH,
+            )
+            copy.start()
+            copies.append(copy)
+        return copies
+
+    flying = [begin(k, 0) for k in range(len(chunks))]
+    for stage in range(len(dims)):
+        for k in range(len(chunks)):
+            for copy in flying[k]:
+                copy.wait()
+            if stage + 1 < len(dims):
+                flying[k] = begin(k, stage + 1)
+
+
+def gather(x, axes, ident):
+    dims = axis_factors(axes)
+    rows, width = x.shape
+    chunks = chunk_orders(dims, width)
+    firsts, slots = slots_of(dims)
+    sizes = tuple(size for _, size, _ in dims)
+    count = math.prod(sizes)
+    nbytes = count * rows * width * x.dtype.itemsize
+    out = pl.pallas_call(
+        functools.partial(gather_kernel, dims, chunks, firsts),
+        out_shape=jax.ShapeDtypeStruct(sizes + (rows, width), x.dtype),
+        in_specs=[pl.BlockSpec(memory_space=pltpu.VMEM)],
+        out_specs=pl.BlockSpec(memory_space=pltpu.VMEM),
+        scratch_shapes=[
+            pltpu.SemaphoreType.DMA((len(chunks), slots)),
+            pltpu.SemaphoreType.DMA((len(chunks), slots)),
+        ],
+        compiler_params=pltpu.CompilerParams(
+            collective_id=ident, has_side_effects=True, vmem_limit_bytes=nbytes + (8 << 20)
+        ),
+        cost_estimate=pl.CostEstimate(flops=0, bytes_accessed=20 * nbytes, transcendentals=0),
+    )(x)
+    return out.reshape(count, rows, width)
+
+
+def scatter_kernel(dims, chunks, firsts, x_ref, o_ref, acc, send_sem, recv_sem, *landed):
+    coords = places(dims)
+    greet(dims, coords)
+    total = len(dims)
+
+    def begin(k, stage):
+        first, columns, order = chunks[k]
+        done = order[:stage]
+        which = order[stage]
+        source = x_ref if stage == 0 else acc
+        copies = []
+        for step in range(1, dims[which][1]):
+            slot = firsts[which] + step - 1
+            target, device = peer(dims, coords, which, step)
+            index = tuple(
+                target if i == which else coords[i] if i in done else pl.ds(0, dims[i][1])
+                for i in range(total)
+            )
+            copy = pltpu.make_async_remote_copy(
+                src_ref=source.at[index + (slice(None), pl.ds(first, columns))],
+                dst_ref=landed[k * total + stage].at[step - 1],
+                send_sem=send_sem.at[k, slot],
+                recv_sem=recv_sem.at[k, slot],
+                device_id=device,
+                device_id_type=MESH,
+            )
+            copy.start()
+            copies.append(copy)
+        return copies
+
+    def add(k, stage):
+        first, columns, order = chunks[k]
+        which = order[stage]
+        remain = [i for i in range(total) if i not in order[: stage + 1]]
+        source = x_ref if stage == 0 else acc
+        got = landed[k * total + stage]
+        count = math.prod(dims[i][1] for i in remain)
+
+        def one(n, carry):
+            inner, left = {}, n
+            for i in reversed(remain):
+                inner[i] = lax.rem(left, dims[i][1])
+                left = left // dims[i][1]
+            index = tuple(inner[i] if i in inner else coords[i] for i in range(total))
+            own = source[index + (slice(None), pl.ds(first, columns))].astype(jnp.float32)
+            for step in range(1, dims[which][1]):
+                place = (step - 1,) + tuple(inner[i] for i in remain)
+                own = own + got[place].astype(jnp.float32)
+            if remain:
+                acc[index + (slice(None), pl.ds(first, columns))] = own.astype(acc.dtype)
+            else:
+                o_ref[:, pl.ds(first, columns)] = own
+            return carry
+
+        if count == 1:
+            one(0, 0)
+        else:
+            lax.fori_loop(0, count, one, 0)
+
+    flying = [begin(k, 0) for k in range(len(chunks))]
+    for stage in range(total):
+        for k in range(len(chunks)):
+            for copy in flying[k]:
+                copy.wait()
+            add(k, stage)
+            if stage + 1 < total:
+                flying[k] = begin(k, stage + 1)
+
+
+def scatter(x, axes, ident):
+    dims = axis_factors(axes)
+    _, rows, width = x.shape
+    chunks = chunk_orders(dims, width)
+    firsts, slots = slots_of(dims)
+    sizes = tuple(size for _, size, _ in dims)
+    landed = []
+    for _, columns, order in chunks:
+        for stage, which in enumerate(order):
+            remain = tuple(sizes[i] for i in range(len(dims)) if i not in order[: stage + 1])
+            landed.append(
+                pltpu.VMEM((sizes[which] - 1,) + remain + (rows, columns), x.dtype)
+            )
+    nbytes = math.prod(sizes) * rows * width * x.dtype.itemsize
+    return pl.pallas_call(
+        functools.partial(scatter_kernel, dims, chunks, firsts),
+        out_shape=jax.ShapeDtypeStruct((rows, width), jnp.float32),
+        in_specs=[pl.BlockSpec(memory_space=pltpu.VMEM)],
+        out_specs=pl.BlockSpec(memory_space=pltpu.VMEM),
+        scratch_shapes=[
+            pltpu.VMEM(sizes + (rows, width), x.dtype),
+            pltpu.SemaphoreType.DMA((len(chunks), slots)),
+            pltpu.SemaphoreType.DMA((len(chunks), slots)),
+            *landed,
+        ],
+        compiler_params=pltpu.CompilerParams(
+            collective_id=ident, has_side_effects=True, vmem_limit_bytes=3 * nbytes + (8 << 20)
+        ),
+        cost_estimate=pl.CostEstimate(flops=0, bytes_accessed=20 * nbytes, transcendentals=0),
+    )(x.reshape(sizes + (rows, width)))
+
+
+def exchange_kernel(parts, x_ref, o_ref, local_sem, send_sem, recv_sem):
+    me = lax.axis_index("dp")
+    other = lax.axis_index("mp")
+    barrier = pltpu.get_barrier_semaphore()
+    for step in range(1, parts):
+        device = (lax.rem(me + step, parts), other)
+        pl.semaphore_signal(barrier, inc=1, device_id=device, device_id_type=MESH)
+    pl.semaphore_wait(barrier, parts - 1)
+    copies = []
+    for step in range(1, parts):
+        target = lax.rem(me + step, parts)
+        copy = pltpu.make_async_remote_copy(
+            src_ref=x_ref.at[target],
+            dst_ref=o_ref.at[me],
+            send_sem=send_sem.at[step - 1],
+            recv_sem=recv_sem.at[step - 1],
+            device_id=(target, other),
+            device_id_type=MESH,
+        )
+        copy.start()
+        copies.append(copy)
+    own = pltpu.make_async_copy(x_ref.at[me], o_ref.at[me], local_sem)
+    own.start()
+    own.wait()
+    for copy in copies:
+        copy.wait()
+
+
+def exchange(x, ident):
+    parts = x.shape[0]
+    return pl.pallas_call(
+        functools.partial(exchange_kernel, parts),
+        out_shape=jax.ShapeDtypeStruct(x.shape, x.dtype),
+        in_specs=[pl.BlockSpec(memory_space=pl.ANY)],
+        out_specs=pl.BlockSpec(memory_space=pl.ANY),
+        scratch_shapes=[
+            pltpu.SemaphoreType.DMA,
+            pltpu.SemaphoreType.DMA((parts - 1,)),
+            pltpu.SemaphoreType.DMA((parts - 1,)),
+        ],
+        compiler_params=pltpu.CompilerParams(collective_id=ident, has_side_effects=True),
+        cost_estimate=pl.CostEstimate(flops=0, bytes_accessed=50 * x.size, transcendentals=0),
+    )(x)
 
 
 def on_device(
@@ -100,7 +372,9 @@
     rows, width = tokens.shape
     share = width // dp
     head_width = query_weight.shape[1]
-    units = gate_weight.shape[1] // dp
+    real_units = gate_weight.shape[1] // dp
+    units = -(-real_units // 128) * 128
+    spare = -(-(share + 1) // 16) * 16 - share
     own_rows = rows // mp
     own = (shard * own_rows, own_rows)
 
@@ -110,7 +384,7 @@
     )
     block = jnp.concatenate([query_weight, key_weight, value_weight, out_weight.T], axis=1)
     gains_row = jnp.pad(gains, (0, block.shape[1] - gains.shape[0]))[None]
-    packed = jnp.concatenate([block, jnp.pad(gains_row, ((0, 15), (0, 0)))], axis=0)
+    packed = jnp.concatenate([block, jnp.pad(gains_row, ((0, spare - 1), (0, 0)))], axis=0)
     packed = lax.all_gather(packed, "dp", axis=0, tiled=False)
     attn_w = packed[:, :share].reshape(width, 4 * head_width)
     qkv_w = attn_w[:, : 3 * head_width]
@@ -123,9 +397,9 @@
     key_g = all_gains[:, 4 * share + gain_head : 4 * share + 2 * gain_head].reshape(head_width)
 
     ffn_block = jnp.stack([gate_weight, up_weight, down_weight.T], axis=0)
-    ffn_block = ffn_block.reshape(3, share, dp, units).transpose(2, 1, 0, 3)
-    ffn_block = ffn_block.reshape(dp, share, 3 * units)
-    ffn_w = lax.all_to_all(ffn_block, "dp", split_axis=0, concat_axis=0, tiled=True)
+    ffn_block = ffn_block.reshape(3, share, dp, real_units).transpose(2, 1, 0, 3)
+    ffn_block = jnp.pad(ffn_block, ((0, 0), (0, 0), (0, 0), (0, units - real_units)))
+    ffn_w = exchange(ffn_block.reshape(dp, share, 3 * units), 3)
     ffn_w = ffn_w.reshape(width, 3 * units)
     glu_w = ffn_w[:, : 2 * units]
     down_wt = ffn_w[:, 2 * units :]
@@ -149,7 +423,7 @@
     attention_low = attention.astype(low)
     attended = matmul(attention_low, value_low).astype(low)
     attn_part = inner_cols(attended, out_wt).astype(low)
-    attn_sum = lax.psum_scatter(attn_part, "mp", scatter_dimension=0, tiled=True).astype(full)
+    attn_sum = scatter(attn_part.reshape(mp, own_rows, width), ("mp",), 4)
 
     inputs_own = lax.dynamic_slice_in_dim(tokens, *own, axis=0).astype(full)
     upstream = lax.dynamic_slice_in_dim(cotangent, *own, axis=0).astype(full)
@@ -161,7 +435,7 @@
     attn_out, back_two = jax.vjp(post_norm, attn_sum, gain_two)
     middle = inputs_own + attn_out
     normed_mid_own, back_three = jax.vjp(normed, middle, gain_three)
-    normed_mid = lax.all_gather(normed_mid_own.astype(low), ("dp", "mp"), axis=0, tiled=True)
+    normed_mid = gather(normed_mid_own.astype(low), ("dp", "mp"), 1).reshape(-1, width)
     glu_pre = matmul(normed_mid, glu_w)
     gate_proj = glu_pre[:, :units]
     up_proj = glu_pre[:, units:]
@@ -172,29 +446,29 @@
     hidden_full, back_glu = jax.vjp(glu, gate_proj, up_proj)
     hidden = hidden_full.astype(low)
     ffn_part = inner_cols(hidden, down_wt).astype(low)
-    ffn_sum = lax.psum_scatter(ffn_part, ("dp", "mp"), scatter_dimension=0, tiled=True).astype(full)
+    ffn_sum = scatter(ffn_part.reshape(dp * mp, own_rows, width), ("dp", "mp"), 2)
     ffn_out, back_four = jax.vjp(post_norm, ffn_sum, gain_four)
     mixed_own = (middle + ffn_out).astype(low)
 
     d_ffn_own, grad_four = back_four(upstream)
-    d_ffn = lax.all_gather(d_ffn_own.astype(low), ("dp", "mp"), axis=0, tiled=True)
+    d_ffn = gather(d_ffn_own.astype(low), ("dp", "mp"), 1).reshape(-1, width)
     grad_down_t = inner_rows(d_ffn, hidden)
     d_hidden = matmul(d_ffn, down_wt)
     d_gate, d_up = back_glu(d_hidden)
     d_glu = jnp.concatenate([d_gate.astype(low), d_up.astype(low)], axis=1)
     d_mid_part = inner_cols(d_glu, glu_w).astype(low)
-    d_mid = lax.psum_scatter(d_mid_part, ("dp", "mp"), scatter_dimension=0, tiled=True).astype(full)
+    d_mid = scatter(d_mid_part.reshape(dp * mp, own_rows, width), ("dp", "mp"), 2)
     grad_glu = inner_rows(normed_mid, d_glu)
     ffn_grad = jnp.concatenate([grad_glu, grad_down_t], axis=1).astype(low)
     ffn_grad = ffn_grad.reshape(dp, share, 3 * units)
-    ffn_grad = lax.all_to_all(ffn_grad, "dp", split_axis=0, concat_axis=0, tiled=True)
-    ffn_grad = ffn_grad.reshape(dp, share, 3, units).transpose(2, 1, 0, 3)
-    ffn_grad = ffn_grad.reshape(3, share, dp * units).astype(full)
+    ffn_grad = exchange(ffn_grad, 3)
+    ffn_grad = ffn_grad.reshape(dp, share, 3, units)[..., :real_units].transpose(2, 1, 0, 3)
+    ffn_grad = ffn_grad.reshape(3, share, dp * real_units).astype(full)
 
     d_mid_add, grad_three = back_three(d_mid)
     d_middle = upstream + d_mid_add
     d_attn_own, grad_two = back_two(d_middle)
-    d_attn = lax.all_gather(d_attn_own.astype(low), "mp", axis=0, tiled=True)
+    d_attn = gather(d_attn_own.astype(low), ("mp",), 5).reshape(rows, width)
 
     grad_out_t = inner_rows(d_attn, attended)
     d_attended = matmul(d_attn, out_wt).astype(low)
@@ -214,7 +488,7 @@
     d_key_pre, grad_kgain = back_key(d_key_rot)
     d_qkv = jnp.concatenate([d_query_pre.astype(low), d_key_pre.astype(low), d_value], axis=1)
     d_in_part = inner_cols(d_qkv, qkv_w).astype(low)
-    d_in = lax.psum_scatter(d_in_part, "mp", scatter_dimension=0, tiled=True).astype(full)
+    d_in = scatter(d_in_part.reshape(mp, own_rows, width), ("mp",), 4)
     grad_qkv = inner_rows(normed_in, d_qkv)
     _, back_one = jax.vjp(normed, inputs_own, gain_one)
     d_in_add, grad_one = back_one(d_in)
@@ -225,18 +499,16 @@
     gains_grad = jnp.pad(gains_grad, ((0, 0), (0, 4 * head_width - gains_grad.shape[1])))
     weights_grad = jnp.concatenate([grad_qkv, grad_out_t], axis=1).reshape(dp, share, 4 * head_width)
     owned = jnp.concatenate(
-        [weights_grad, jnp.pad(gains_grad[:, None], ((0, 0), (0, 15), (0, 0)))], axis=1
+        [weights_grad, jnp.pad(gains_grad[:, None], ((0, 0), (0, spare - 1), (0, 0)))], axis=1
     ).astype(low)
-    owned = lax.psum_scatter(owned, "dp", scatter_dimension=0, tiled=True)[0].astype(full)
+    owned = scatter(owned, ("dp",), 6)
+    gains_back = jnp.pad(owned[share].reshape(2, 2 * head_width), ((0, spare), (0, 0)))[:spare]
     shared = jnp.concatenate(
-        [
-            owned[:share, head_width : 3 * head_width].reshape(-1),
-            owned[share, : 4 * share + 2 * gain_head],
-        ]
-    )
-    shared = lax.psum(shared, "mp")
-    kv_grad = shared[: 2 * share * head_width].reshape(share, 2 * head_width)
-    gain_out = shared[2 * share * head_width :]
+        [owned[:share, head_width : 3 * head_width], gains_back], axis=0
+    )
+    shared = jnp.sum(gather(shared.astype(low), ("mp",), 7).astype(full), axis=0)
+    kv_grad = shared[:share]
+    gain_out = shared[share : share + 2].reshape(-1)
     mixed = lax.all_gather(mixed_own, "mp", axis=0, tiled=True)
     tokens_grad = lax.all_gather(tokens_grad_own.astype(low), "mp", axis=0, tiled=True).astype(full)
     return (
@@ -254,7 +526,7 @@
         gain_out[2 * share : 3 * share],
         gain_out[3 * share : 4 * share],
         gain_out[4 * share : 4 * share + gain_head],
-        gain_out[4 * share + gain_head :],
+        gain_out[4 * share + gain_head : 4 * share + 2 * gain_head],
     )
 
 

time: 654 us -> 474 us (0.72)
  waiting for transfers between devices: 378 us -> 0.04 us
  Pallas kernels: 0 us -> 313 us
  blocking collectives: 140 us -> 13.7 us
  local copies, waits for them, and re-layouts: 54 us -> 69.3 us
    pallas_call x0 -> x11, Pallas kernels: none -> 313 us  [the longest x5 126 us: scatter(): pl.pallas_call(functools.partial(scatter_kernel, dims, chunks, firsts), o...]
    reduce_scatter x5 -> x0, waiting for transfers between devices: 235 us -> none  [the longest x1 102 us: on_device(): lax.psum_scatter(ffn_part, ('dp', 'mp'), scatter_dimension=0, tiled=True)]
    all_to_all x2 -> x0, blocking collectives: 117 us -> none  [the longest x1 59.2 us: on_device(): lax.all_to_all(ffn_grad, 'dp', split_axis=0, concat_axis=0, tiled=True)]
    all_gather x2 -> x0, waiting for transfers between devices: 60.8 us -> none  [the longest x1 60.8 us: on_device(): lax.all_gather(d_ffn_own.astype(low), ('dp', 'mp'), axis=0, tiled=True)]
    all_gather x1, waiting for transfers between devices: 50.8 us -> 0.02 us  [on_device(): packed = lax.all_gather(packed, 'dp', axis=0, tiled=False)]
    psum x1 -> x0, waiting for transfers between devices: 30.8 us -> none  [on_device(): shared = lax.psum(shared, 'mp')]
    all_gather x1 -> x0, blocking collectives: 8.91 us -> none  [on_device(): d_attn = lax.all_gather(d_attn_own.astype(low), 'mp', axis=0, tiled=True)]
    dot_general x0 -> x2, local copies, waits for them, and re-layouts: none -> 7.38 us  [inner_rows(): lax.dot_general(left_op, right_op, (((0,), (0,)), ((), ())), preferred_el...]
  transfers between devices with their start and end apart: 9 -> 1, of which waited for: 7 -> 0; matrix products, arithmetic and copies ran while one was open for 9% -> 4% of each run, Pallas kernels for 0% -> 14%
where the time goes in v2:
time: 474 us; the launch traced here: 469 us
  Pallas kernels  313 us (66%)
  local copies, waits for them, and re-layouts  69.3 us (15%)
  other arithmetic  31.4 us (7%)
  matrix products  25.4 us (5%)
  between operations  15.9 us (3%)
  blocking collectives  13.7 us (3%)
    pallas_call x5, Pallas kernels, scatter(): pl.pallas_call(functools.partial(scatter_kernel, dims, chunks, firsts), o...  126 us
    pallas_call x2, Pallas kernels, exchange(): pl.pallas_call(functools.partial(exchange_kernel, parts), out_shape=jax.S...  108 us
    pallas_call x4, Pallas kernels, gather(): pl.pallas_call(functools.partial(gather_kernel, dims, chunks, firsts), ou...  79.8 us
    dot_general x6, matrix products, inner_rows(): lax.dot_general(left_op, right_op, (((0,), (0,)), ((), ())), preferred_el...  10.6 us
  transfers between devices with their start and end apart: 1, of which 0 were waited for; matrix products, arithmetic and copies ran while one was open for 4% of the time, Pallas kernels for 14%

profile of v2, /device:TPU:13, one launch (start us, length us, event | category | flops | bytes accessed | tf_op | source)
XLA Modules:
  0.0 469.2 jit_solution(15642287889349868909)
XLA Ops:
  7.2 4.1 concatenate.51
  11.3 1.8 fusion.29
  15.0 2.0 stack.12
  21.6 4.6 maximum_bitcast_fusion
  27.4 3.5 reshape.328.x_ref
  31.0 64.9 %shard_map.273 = bf16[8,144,768]{2,1,0:T(8,128)(2,1)} custom-call(bf16[8,144,768]{2,1,0:T(8,128)(2,1)} %reshape.328.x_ref), custom_call_target="tpu_custom_call" | custom-call | bytes 44236800 | tf_op jit(solution)/shard_map/pallas_call | solution.py:334
  97.2 2.0 slice.168
  104.0 6.7 %shard_map.271 = f32[48,1152]{1,0:T(8,128)S(1)} custom-call(bf16[2,2,48,1152]{3,2,1,0:T(8,128)(2,1)S(1)} %bitcast.70), custom_call_target="tpu_custom_call" | custom-call | bytes 8847360 | tf_op jit(solution)/shard_map/pallas_call | solution.py:286
  112.6 32.4 %shard_map.272 = bf16[4,2,2,2,48,1152]{5,4,3,2,1,0:T(8,128)(2,1)S(1)} custom-call(bf16[48,1152]{1,0:T(8,128)(2,1)S(1)} %multiply_convert_fusion.2.x_ref), custom_call_target="tpu_custom_call" | custom-call | bytes 70778880 | tf_op jit(solution)/shard_map/pallas_call | solution.py:186
  145.0 2.3 fusion.17
  150.2 33.3 %shard_map.274 = f32[48,1152]{1,0:T(8,128)S(1)} custom-call(bf16[4,2,2,2,48,1152]{5,4,3,2,1,0:T(8,128)(2,1)S(1)} %bitcast.62), custom_call_target="tpu_custom_call" | custom-call | bytes 70778880 | tf_op jit(solution)/shard_map/pallas_call | solution.py:286
  185.4 1.4 mul.587
  186.8 1.7 fusion.35
  189.1 1.9 fusion.36
  191.1 31.6 %shard_map.275 = bf16[4,2,2,2,48,1152]{5,4,3,2,1,0:T(8,128)(2,1)S(1)} custom-call(bf16[48,1152]{1,0:T(8,128)(2,1)S(1)} %get-tuple-element.50.x_ref), custom_call_target="tpu_custom_call" | custom-call | bytes 70778880 | tf_op jit(solution)/shard_map/pallas_call | solution.py:186
  222.7 5.3 %fusion.6 = (bf16[1536,256]{0,1:T(8,128)(2,1)S(1)}, bf16[1536,256]{0,1:T(8,128)(2,1)S(1)}) fusion(f32[1536,512]{0,1:T(8,128)} %copy-done.18, bf16[1536,1152]{1,0:T(8,128)(2,1)S(1)} %bitcast.65, bf16[1152,768]{1,0:T(8,128)(2,1)S(1)} %bitcast.81), kind=kOutput, calls=%fused_computation.19 | convolution fusion | flops 915406848 | bytes 8847360 | tf_op jit(solution)/shard_map/dot_general | solution.py:20
  228.1 2.2 convolution_convert_fusion.1
  230.4 34.4 %shard_map.276 = f32[48,1152]{1,0:T(8,128)S(1)} custom-call(bf16[4,2,2,2,48,1152]{5,4,3,2,1,0:T(8,128)(2,1)S(1)} %bitcast.67), custom_call_target="tpu_custom_call" | custom-call | bytes 70778880 | tf_op jit(solution)/shard_map/pallas_call | solution.py:286
  265.6 1.7 multiply_reduce_fusion.1
  268.2 7.6 %shard_map.277 = bf16[2,2,48,1152]{3,2,1,0:T(8,128)(2,1)S(1)} custom-call(bf16[48,1152]{1,0:T(8,128)(2,1)S(1)} %fusion.37.x_ref), custom_call_target="tpu_custom_call" | custom-call | bytes 8847360 | tf_op jit(solution)/shard_map/pallas_call | solution.py:186
  279.8 1.5 convolution_convert_fusion.5
  281.4 1.6 pad_maximum_fusion.1
  283.0 4.3 copy.66
  288.3 6.3 %shard_map.278 = f32[48,1152]{1,0:T(8,128)S(1)} custom-call(bf16[2,2,48,1152]{3,2,1,0:T(8,128)(2,1)S(1)} %bitcast.71), custom_call_target="tpu_custom_call" | custom-call | bytes 8847360 | tf_op jit(solution)/shard_map/pallas_call | solution.py:286
  295.3 1.7 fusion.43
  297.0 1.4 reshape.330
  299.7 1.3 reshape.335
  301.0 1.4 reshape.331
  303.1 1.4 concatenate.59
  305.3 2.0 pad_maximum_fusion.x_ref
  307.3 45.4 %shard_map.279 = f32[160,1024]{1,0:T(8,128)S(1)} custom-call(bf16[4,2,160,1024]{3,2,1,0:T(8,128)(2,1)S(1)} %pad_maximum_fusion.x_ref), custom_call_target="tpu_custom_call" | custom-call | bytes 52428800 | tf_op jit(solution)/shard_map/pallas_call | solution.py:286
  355.2 8.2 %shard_map.280 = bf16[2,2,160,512]{3,2,1,0:T(8,128)(2,1)S(1)} custom-call(bf16[160,512]{1,0:T(8,128)(2,1)S(1)} %pad_maximum_fusion.7.x_ref), custom_call_target="tpu_custom_call" | custom-call | bytes 13107200 | tf_op jit(solution)/shard_map/pallas_call | solution.py:186
  365.5 1.7 slice_bitcast_fusion
  367.2 3.8 copy.68
  371.0 5.7 %fusion.12 = bf16[8,144,512]{2,1,0:T(8,128)(2,1)} fusion(bf16[8,144,1536]{2,1,0:T(8,128)(2,1)} %bitcast.77, bf16[1536,256]{0,1:T(8,128)(2,1)} %copy-done.81, bf16[1536,256]{0,1:T(8,128)(2,1)} %copy-done.80), kind=kOutput, calls=%fused_computation.28 | convolution fusion | flops 1815674880 | bytes 6291456 | tf_op jit(solution)/shard_map/dot_general | solution.py:24
  376.7 3.6 copy.70
  380.3 3.4 convolution_convert_fusion.6
  383.7 1.4 pad_maximum_fusion.2.x_ref
  385.1 42.7 %shard_map.281 = bf16[8,144,768]{2,1,0:T(8,128)(2,1)} custom-call(bf16[8,144,768]{2,1,0:T(8,128)(2,1)} %pad_maximum_fusion.2.x_ref), custom_call_target="tpu_custom_call" | custom-call | bytes 44236800 | tf_op jit(solution)/shard_map/pallas_call | solution.py:334
  427.8 3.4 reshape.336
  431.9 2.5 fusion.106
  434.4 1.7 copy.74
  436.1 2.7 squeeze.12
  438.8 1.7 copy.72
  440.5 2.7 squeeze.10
  443.9 1.4 squeeze.11
  446.5 6.8 %all_gather.15 = bf16[192,1152]{1,0:T(8,128)(2,1)S(1)} all-gather(bf16[48,1152]{1,0:T(8,128)(2,1)S(1)} %fusion.39), channel_id=1, replica_groups=mesh['dp'=8,'mp'=4] {'mp'}, dimensions={0}, use_global_device_ids=true | all-gather | bytes 552960 | tf_op jit(solution)/shard_map/all_gather | solution.py:513
  454.3 6.8 %all_gather.14 = bf16[192,1152]{1,0:T(8,128)(2,1)S(1)} all-gather(bf16[48,1152]{1,0:T(8,128)(2,1)S(1)} %copy-done.28), channel_id=1, replica_groups=mesh['dp'=8,'mp'=4] {'mp'}, dimensions={0}, use_global_device_ids=true | all-gather | bytes 552960 | tf_op jit(solution)/shard_map/all_gather | solution.py:512
  (258 shorter events, 39.1 us)
Async XLA Ops:
  7.2 89.1 %all-gather.3.cloned.1.call-start = ((), (), s32[]{:S(2)}) async-start(), calls=%async_computation | async-start | bytes 2949120 | tf_op jit(solution)/shard_map/all_gather | solution.py:388
  13.1 4.8 %copy-start.26 = (bf16[144,1728]{1,0:T(8,128)(2,1)S(1)}, bf16[144,1728]{1,0:T(8,128)(2,1)}, u32[]{:S(2)}) copy-start(bf16[144,1728]{1,0:T(8,128)(2,1)} %param.24) | copy-start | bytes 1492996
  17.9 1.9 copy-start.27
  31.0 65.0 %copy-start.21 = (bf16[192,1152]{1,0:T(8,128)(2,1)S(1)}, bf16[192,1152]{1,0:T(8,128)(2,1)}, u32[]{:S(2)}) copy-start(bf16[192,1152]{1,0:T(8,128)(2,1)} %param.16) | copy-start | bytes 1327108
  96.0 15.1 %copy-start.51 = (f32[48]{0:T(128)}, f32[48]{0:T(128)S(1)}, u32[]{:S(2)}) copy-start(f32[48]{0:T(128)S(1)} %dynamic_slice.10) | copy-start | bytes 580
  96.0 5.9 %copy-start.69 = (f32[128]{0:T(128)}, f32[128]{0:T(128)S(1)}, u32[]{:S(2)}) copy-start(f32[128]{0:T(128)S(1)} %multiply_power_fusion) | copy-start | bytes 1540
  96.2 4.0 copy-start.71
  96.2 5.7 %copy-start.53 = (f32[192]{0:T(256)}, f32[192]{0:T(256)S(1)}, u32[]{:S(2)}) copy-start(f32[192]{0:T(256)S(1)} %fusion.88) | copy-start | bytes 2308
  99.2 4.4 copy-start.14
  100.8 2.8 copy-start.12
  101.6 2.4 copy-start.47
  101.6 2.4 copy-start.49
  101.7 2.3 copy-start.43
  101.8 2.2 copy-start.45
  102.7 9.1 %copy-start.63 = (f32[192]{0:T(256)}, f32[192]{0:T(256)S(1)}, u32[]{:S(2)}) copy-start(f32[192]{0:T(256)S(1)} %get-tuple-element.76) | copy-start | bytes 2308
  103.4 8.4 %copy-start.65 = (f32[192]{0:T(256)}, f32[192]{0:T(256)S(1)}, u32[]{:S(2)}) copy-start(f32[192]{0:T(256)S(1)} %fusion.49) | copy-start | bytes 2308
  103.6 7.2 %copy-start.29 = (bf16[192,256]{1,0:T(8,128)(2,1)}, bf16[192,256]{1,0:T(8,128)(2,1)S(1)}, u32[]{:S(2)}) copy-start(bf16[192,256]{1,0:T(8,128)(2,1)S(1)} %convolution_convert_fusion.9) | copy-start | bytes 294916
  112.6 32.4 %copy-start.16 = (bf16[8,144,768]{2,1,0:T(8,128)(2,1)S(1)}, bf16[8,144,768]{2,1,0:T(8,128)(2,1)}, u32[]{:S(2)}) copy-start(bf16[8,144,768]{2,1,0:T(8,128)(2,1)} %shard_map.273) | copy-start | bytes 5308420
  191.1 31.6 %copy-start.17 = (bf16[8,144,768]{2,1,0:T(8,128)(2,1)S(1)}, bf16[8,144,768]{2,1,0:T(8,128)(2,1)}, u32[]{:S(2)}) copy-start(bf16[8,144,768]{2,1,0:T(8,128)(2,1)} %shard_map.273) | copy-start | bytes 5308420
  222.7 5.4 %copy-start = (bf16[4,2,2,2,48,1152]{5,4,3,2,1,0:T(8,128)(2,1)}, bf16[4,2,2,2,48,1152]{5,4,3,2,1,0:T(8,128)(2,1)S(1)}, u32[]{:S(2)}) copy-start(bf16[4,2,2,2,48,1152]{5,4,3,2,1,0:T(8,128)(2,1)S(1)} %shard_map.275) | copy-start | bytes 10616836
  228.0 2.3 copy-start.80
  228.1 2.3 copy-start.81
  230.3 34.5 %copy-start.11 = (f32[48,1152]{1,0:T(8,128)S(1)}, f32[48,1152]{1,0:T(8,128)}, u32[]{:S(2)}) copy-start(f32[48,1152]{1,0:T(8,128)} %copy-done.10) | copy-start | bytes 663556
  230.3 34.5 %copy-start.62 = (f32[48]{0:T(128)S(1)}, f32[48]{0:T(128)}, u32[]{:S(2)}) copy-start(f32[48]{0:T(128)} %copy-done.61) | copy-start | bytes 580
  230.4 35.2 %copy-start.78 = (f32[48]{0:T(128)S(1)}, f32[48]{0:T(128)}, u32[]{:S(2)}) copy-start(f32[48]{0:T(128)} %copy-done.77) | copy-start | bytes 580
  230.4 35.2 %copy-start.3 = (f32[48,1152]{1,0:T(8,128)S(1)}, f32[48,1152]{1,0:T(8,128)}, u32[]{:S(2)}) copy-start(f32[48,1152]{1,0:T(8,128)} %copy-done.2) | copy-start | bytes 663556
  230.4 35.2 %copy-start.52 = (f32[48]{0:T(128)S(1)}, f32[48]{0:T(128)}, u32[]{:S(2)}) copy-start(f32[48]{0:T(128)} %copy-done.51) | copy-start | bytes 580
  230.4 35.2 %copy-start.60 = (f32[48]{0:T(128)S(1)}, f32[48]{0:T(128)}, u32[]{:S(2)}) copy-start(f32[48]{0:T(128)} %copy-done.59) | copy-start | bytes 580
  230.4 37.0 %copy-start.76 = (f32[48]{0:T(128)S(1)}, f32[48]{0:T(128)}, u32[]{:S(2)}) copy-start(f32[48]{0:T(128)} %copy-done.75) | copy-start | bytes 580
  264.8 11.0 %copy-start.15 = (bf16[8,144,1024]{2,1,0:T(8,128)(2,1)S(1)}, bf16[8,144,1024]{2,1,0:T(8,128)(2,1)}, u32[]{:S(2)}) copy-start(bf16[8,144,1024]{2,1,0:T(8,128)(2,1)} %copy-done.14) | copy-start | bytes 7077892
  265.6 10.6 %copy-start.13 = (f32[192,768]{1,0:T(8,128)S(1)}, f32[192,768]{1,0:T(8,128)}, u32[]{:S(2)}) copy-start(f32[192,768]{1,0:T(8,128)} %copy-done.12) | copy-start | bytes 1769476
  265.6 10.6 %copy-start.25 = (f32[192,192]{0,1:T(8,128)S(1)}, f32[192,192]{0,1:T(8,128)}, u32[]{:S(2)}) copy-start(f32[192,192]{0,1:T(8,128)} %copy-done.24) | copy-start | bytes 442372
  265.6 10.6 %copy-start.64 = (f32[192]{0:T(256)S(1)}, f32[192]{0:T(256)}, u32[]{:S(2)}) copy-start(f32[192]{0:T(256)} %copy-done.63) | copy-start | bytes 2308
  265.6 10.6 %copy-start.66 = (f32[192]{0:T(256)S(1)}, f32[192]{0:T(256)}, u32[]{:S(2)}) copy-start(f32[192]{0:T(256)} %copy-done.65) | copy-start | bytes 2308
  268.2 8.4 %copy-start.36 = (bf16[192,128]{1,0:T(8,128)(2,1)S(1)}, bf16[192,128]{1,0:T(8,128)(2,1)}, u32[]{:S(2)}) copy-start(bf16[192,128]{1,0:T(8,128)(2,1)} %copy-done.35) | copy-start | bytes 147460
  268.2 8.4 %copy-start.38 = (bf16[192,128]{1,0:T(8,128)(2,1)S(1)}, bf16[192,128]{1,0:T(8,128)(2,1)}, u32[]{:S(2)}) copy-start(bf16[192,128]{1,0:T(8,128)(2,1)} %copy-done.37) | copy-start | bytes 147460
  268.2 8.6 %copy-start.32 = (bf16[192,128]{1,0:T(8,128)(2,1)S(1)}, bf16[192,128]{1,0:T(8,128)(2,1)}, u32[]{:S(2)}) copy-start(bf16[192,128]{1,0:T(8,128)(2,1)} %copy-done.31) | copy-start | bytes 147460
  268.2 8.6 %copy-start.34 = (bf16[192,128]{1,0:T(8,128)(2,1)S(1)}, bf16[192,128]{1,0:T(8,128)(2,1)}, u32[]{:S(2)}) copy-start(bf16[192,128]{1,0:T(8,128)(2,1)} %copy-done.33) | copy-start | bytes 147460
  283.0 19.4 %copy-start.42 = (bf16[1152]{0:T(1024)(128)(2,1)S(1)}, bf16[1152]{0:T(1024)(128)(2,1)}, u32[]{:S(2)}) copy-start(bf16[1152]{0:T(1024)(128)(2,1)} %get-tuple-element.29) | copy-start | bytes 6916
  283.0 20.1 %copy-start.41 = (bf16[1152]{0:T(1024)(128)(2,1)S(1)}, bf16[1152]{0:T(1024)(128)(2,1)}, u32[]{:S(2)}) copy-start(bf16[1152]{0:T(1024)(128)(2,1)} %get-tuple-element.19) | copy-start | bytes 6916
  371.0 5.7 %copy-start.1 = (bf16[4,2,2,2,48,1152]{5,4,3,2,1,0:T(8,128)(2,1)S(1)}, bf16[4,2,2,2,48,1152]{5,4,3,2,1,0:T(8,128)(2,1)}, u32[]{:S(2)}) copy-start(bf16[4,2,2,2,48,1152]{5,4,3,2,1,0:T(8,128)(2,1)} %copy-done) | copy-start | bytes 10616836
  380.3 3.4 copy-start.23
  443.2 2.2 copy-start.73
  443.2 2.2 copy-start.74
  443.2 2.2 copy-start.7
  443.2 2.2 copy-start.20
  443.2 2.2 copy-start.68
  445.4 8.9 %copy-start.28 = (bf16[48,1152]{1,0:T(8,128)(2,1)S(1)}, bf16[48,1152]{1,0:T(8,128)(2,1)}, u32[]{:S(2)}) copy-start(bf16[48,1152]{1,0:T(8,128)(2,1)} %get-tuple-element.51) | copy-start | bytes 331780
  (35 other events, 38.0 us)
Sparse Core Ops, SparseCore 0:
  13.2 80.6 all-gather.2

commit v3 on v2

--- a/solution.py
+++ b/solution.py
@@ -117,10 +117,16 @@
     return target, (device["dp"], device["mp"])
 
 
-def greet(dims, coords):
+def greet(dims, coords, parts=0):
     barrier = pltpu.get_barrier_semaphore()
     count = 0
-    for which, (_, size, _) in enumerate(dims):
+    for step in range(1, parts):
+        device = (lax.rem(lax.axis_index("dp") + step, parts), lax.axis_index("mp"))
+        pl.semaphore_signal(barrier, inc=1, device_id=device, device_id_type=MESH)
+        count += 1
+    for which, (axis, size, _) in enumerate(dims):
+        if parts and axis == "dp":
+            continue
         for step in range(1, size):
             _, device = peer(dims, coords, which, step)
             pl.semaphore_signal(barrier, inc=1, device_id=device, device_id_type=MESH)
@@ -136,10 +142,44 @@
     return firsts, total
 
 
-def gather_kernel(dims, chunks, firsts, x_ref, o_ref, send_sem, recv_sem):
+def start_exchange(parts, x_ref, o_ref, local_sem, send_sem, recv_sem):
+    me = lax.axis_index("dp")
+    other = lax.axis_index("mp")
+    copies = []
+    for step in range(1, parts):
+        target = lax.rem(me + step, parts)
+        copy = pltpu.make_async_remote_copy(
+            src_ref=x_ref.at[target],
+            dst_ref=o_ref.at[me],
+            send_sem=send_sem.at[step - 1],
+            recv_sem=recv_sem.at[step - 1],
+            device_id=(target, other),
+            device_id_type=MESH,
+        )
+        copy.start()
+        copies.append(copy)
+    own = pltpu.make_async_copy(x_ref.at[me], o_ref.at[me], local_sem)
+    own.start()
+    copies.append(own)
+    return copies
+
+
+def exchange_scratch(parts):
+    return [
+        pltpu.SemaphoreType.DMA,
+        pltpu.SemaphoreType.DMA((parts - 1,)),
+        pltpu.SemaphoreType.DMA((parts - 1,)),
+    ]
+
+
+def gather_kernel(dims, chunks, firsts, parts, *refs):
+    if parts:
+        x_ref, ex_ref, o_ref, eo_ref, send_sem, recv_sem, *exchange_sems = refs
+    else:
+        x_ref, o_ref, send_sem, recv_sem = refs
     coords = places(dims)
     o_ref[tuple(coords)] = x_ref[...]
-    greet(dims, coords)
+    greet(dims, coords, parts)
 
     def begin(k, stage):
         first, columns, order = chunks[k]
@@ -167,15 +207,18 @@
         return copies
 
     flying = [begin(k, 0) for k in range(len(chunks))]
+    moving = start_exchange(parts, ex_ref, eo_ref, *exchange_sems) if parts else []
     for stage in range(len(dims)):
         for k in range(len(chunks)):
             for copy in flying[k]:
                 copy.wait()
             if stage + 1 < len(dims):
                 flying[k] = begin(k, stage + 1)
-
-
-def gather(x, axes, ident):
+    for copy in moving:
+        copy.wait()
+
+
+def gather(x, axes, ident, extra=None):
     dims = axis_factors(axes)
     rows, width = x.shape
     chunks = chunk_orders(dims, width)
@@ -183,26 +226,37 @@
     sizes = tuple(size for _, size, _ in dims)
     count = math.prod(sizes)
     nbytes = count * rows * width * x.dtype.itemsize
-    out = pl.pallas_call(
-        functools.partial(gather_kernel, dims, chunks, firsts),
-        out_shape=jax.ShapeDtypeStruct(sizes + (rows, width), x.dtype),
-        in_specs=[pl.BlockSpec(memory_space=pltpu.VMEM)],
-        out_specs=pl.BlockSpec(memory_space=pltpu.VMEM),
+    more = [] if extra is None else [extra]
+    parts = extra.shape[0] if more else 0
+    anywhere = [pl.BlockSpec(memory_space=pl.ANY)] * len(more)
+    out, *moved = pl.pallas_call(
+        functools.partial(gather_kernel, dims, chunks, firsts, parts),
+        out_shape=[jax.ShapeDtypeStruct(sizes + (rows, width), x.dtype)]
+        + [jax.ShapeDtypeStruct(e.shape, e.dtype) for e in more],
+        in_specs=[pl.BlockSpec(memory_space=pltpu.VMEM)] + anywhere,
+        out_specs=[pl.BlockSpec(memory_space=pltpu.VMEM)] + anywhere,
         scratch_shapes=[
             pltpu.SemaphoreType.DMA((len(chunks), slots)),
             pltpu.SemaphoreType.DMA((len(chunks), slots)),
+            *(exchange_scratch(parts) if more else []),
         ],
         compiler_params=pltpu.CompilerParams(
             collective_id=ident, has_side_effects=True, vmem_limit_bytes=nbytes + (8 << 20)
         ),
         cost_estimate=pl.CostEstimate(flops=0, bytes_accessed=20 * nbytes, transcendentals=0),
-    )(x)
-    return out.reshape(count, rows, width)
-
-
-def scatter_kernel(dims, chunks, firsts, x_ref, o_ref, acc, send_sem, recv_sem, *landed):
+    )(x, *more)
+    out = out.reshape(count, rows, width)
+    return (out, moved[0]) if more else out
+
+
+def scatter_kernel(dims, chunks, firsts, parts, *refs):
+    if parts:
+        x_ref, ex_ref, o_ref, eo_ref, acc, send_sem, recv_sem = refs[:7]
+        exchange_sems, landed = refs[7:10], refs[10:]
+    else:
+        x_ref, o_ref, acc, send_sem, recv_sem, *landed = refs
     coords = places(dims)
-    greet(dims, coords)
+    greet(dims, coords, parts)
     total = len(dims)
 
     def begin(k, stage):
@@ -260,6 +314,7 @@
             lax.fori_loop(0, count, one, 0)
 
     flying = [begin(k, 0) for k in range(len(chunks))]
+    moving = start_exchange(parts, ex_ref, eo_ref, *exchange_sems) if parts else []
     for stage in range(total):
         for k in range(len(chunks)):
             for copy in flying[k]:
@@ -267,9 +322,11 @@
             add(k, stage)
             if stage + 1 < total:
                 flying[k] = begin(k, stage + 1)
-
-
-def scatter(x, axes, ident):
+    for copy in moving:
+        copy.wait()
+
+
+def scatter(x, axes, ident, extra=None):
     dims = axis_factors(axes)
     _, rows, width = x.shape
     chunks = chunk_orders(dims, width)
@@ -283,67 +340,28 @@
                 pltpu.VMEM((sizes[which] - 1,) + remain + (rows, columns), x.dtype)
             )
     nbytes = math.prod(sizes) * rows * width * x.dtype.itemsize
-    return pl.pallas_call(
-        functools.partial(scatter_kernel, dims, chunks, firsts),
-        out_shape=jax.ShapeDtypeStruct((rows, width), jnp.float32),
-        in_specs=[pl.BlockSpec(memory_space=pltpu.VMEM)],
-        out_specs=pl.BlockSpec(memory_space=pltpu.VMEM),
+    more = [] if extra is None else [extra]
+    parts = extra.shape[0] if more else 0
+    anywhere = [pl.BlockSpec(memory_space=pl.ANY)] * len(more)
+    out, *moved = pl.pallas_call(
+        functools.partial(scatter_kernel, dims, chunks, firsts, parts),
+        out_shape=[jax.ShapeDtypeStruct((rows, width), jnp.float32)]
+        + [jax.ShapeDtypeStruct(e.shape, e.dtype) for e in more],
+        in_specs=[pl.BlockSpec(memory_space=pltpu.VMEM)] + anywhere,
+        out_specs=[pl.BlockSpec(memory_space=pltpu.VMEM)] + anywhere,
         scratch_shapes=[
             pltpu.VMEM(sizes + (rows, width), x.dtype),
             pltpu.SemaphoreType.DMA((len(chunks), slots)),
             pltpu.SemaphoreType.DMA((len(chunks), slots)),
+            *(exchange_scratch(parts) if more else []),
             *landed,
         ],
         compiler_params=pltpu.CompilerParams(
             collective_id=ident, has_side_effects=True, vmem_limit_bytes=3 * nbytes + (8 << 20)
         ),
         cost_estimate=pl.CostEstimate(flops=0, bytes_accessed=20 * nbytes, transcendentals=0),
-    )(x.reshape(sizes + (rows, width)))
-
-
-def exchange_kernel(parts, x_ref, o_ref, local_sem, send_sem, recv_sem):
-    me = lax.axis_index("dp")
-    other = lax.axis_index("mp")
-    barrier = pltpu.get_barrier_semaphore()
-    for step in range(1, parts):
-        device = (lax.rem(me + step, parts), other)
-        pl.semaphore_signal(barrier, inc=1, device_id=device, device_id_type=MESH)
-    pl.semaphore_wait(barrier, parts - 1)
-    copies = []
-    for step in range(1, parts):
-        target = lax.rem(me + step, parts)
-        copy = pltpu.make_async_remote_copy(
-            src_ref=x_ref.at[target],
-            dst_ref=o_ref.at[me],
-            send_sem=send_sem.at[step - 1],
-            recv_sem=recv_sem.at[step - 1],
-            device_id=(target, other),
-            device_id_type=MESH,
-        )
-        copy.start()
-        copies.append(copy)
-    own = pltpu.make_async_copy(x_ref.at[me], o_ref.at[me], local_sem)
-    own.start()
-    own.wait()
-    for copy in copies:
-        copy.wait()
-
-
-def exchange(x, ident):
-    parts = x.shape[0]
-    return pl.pallas_call(
-        functools.partial(exchange_kernel, parts),
-        out_shape=jax.ShapeDtypeStruct(x.shape, x.dtype),
-        in_specs=[pl.BlockSpec(memory_space=pl.ANY)],
-        out_specs=pl.BlockSpec(memory_space=pl.ANY),
-        scratch_shapes=[
-            pltpu.SemaphoreType.DMA,
-            pltpu.SemaphoreType.DMA((parts - 1,)),
-            pltpu.SemaphoreType.DMA((parts - 1,)),
-        ],
-        compiler_params=pltpu.CompilerParams(collective_id=ident, has_side_effects=True),
-        cost_estimate=pl.CostEstimate(flops=0, bytes_accessed=50 * x.size, transcendentals=0),
-    )(x)
+    )(x.reshape(sizes + (rows, width)), *more)
+    return (out, moved[0]) if more else out
 
 
 def on_device(
@@ -385,7 +403,7 @@
     block = jnp.concatenate([query_weight, key_weight, value_weight, out_weight.T], axis=1)
     gains_row = jnp.pad(gains, (0, block.shape[1] - gains.shape[0]))[None]
     packed = jnp.concatenate([block, jnp.pad(gains_row, ((0, spare - 1), (0, 0)))], axis=0)
-    packed = lax.all_gather(packed, "dp", axis=0, tiled=False)
+    packed = gather(packed, ("dp",), 10)
     attn_w = packed[:, :share].reshape(width, 4 * head_width)
     qkv_w = attn_w[:, : 3 * head_width]
     out_wt = attn_w[:, 3 * head_width :]
@@ -399,10 +417,7 @@
     ffn_block = jnp.stack([gate_weight, up_weight, down_weight.T], axis=0)
     ffn_block = ffn_block.reshape(3, share, dp, real_units).transpose(2, 1, 0, 3)
     ffn_block = jnp.pad(ffn_block, ((0, 0), (0, 0), (0, 0), (0, units - real_units)))
-    ffn_w = exchange(ffn_block.reshape(dp, share, 3 * units), 3)
-    ffn_w = ffn_w.reshape(width, 3 * units)
-    glu_w = ffn_w[:, : 2 * units]
-    down_wt = ffn_w[:, 2 * units :]
+    ffn_block = ffn_block.reshape(dp, share, 3 * units)
 
     inputs = tokens.astype(full)
     position, live_rows, allowed = layout(doc_lengths, rows // doc_lengths.shape[0])
@@ -435,7 +450,11 @@
     attn_out, back_two = jax.vjp(post_norm, attn_sum, gain_two)
     middle = inputs_own + attn_out
     normed_mid_own, back_three = jax.vjp(normed, middle, gain_three)
-    normed_mid = gather(normed_mid_own.astype(low), ("dp", "mp"), 1).reshape(-1, width)
+    normed_mid, ffn_w = gather(normed_mid_own.astype(low), ("dp", "mp"), 8, ffn_block)
+    normed_mid = normed_mid.reshape(-1, width)
+    ffn_w = ffn_w.reshape(width, 3 * units)
+    glu_w = ffn_w[:, : 2 * units]
+    down_wt = ffn_w[:, 2 * units :]
     glu_pre = matmul(normed_mid, glu_w)
     gate_proj = glu_pre[:, :units]
     up_proj = glu_pre[:, units:]
@@ -457,11 +476,12 @@
     d_gate, d_up = back_glu(d_hidden)
     d_glu = jnp.concatenate([d_gate.astype(low), d_up.astype(low)], axis=1)
     d_mid_part = inner_cols(d_glu, glu_w).astype(low)
-    d_mid = scatter(d_mid_part.reshape(dp * mp, own_rows, width), ("dp", "mp"), 2)
     grad_glu = inner_rows(normed_mid, d_glu)
     ffn_grad = jnp.concatenate([grad_glu, grad_down_t], axis=1).astype(low)
     ffn_grad = ffn_grad.reshape(dp, share, 3 * units)
-    ffn_grad = exchange(ffn_grad, 3)
+    d_mid, ffn_grad = scatter(
+        d_mid_part.reshape(dp * mp, own_rows, width), ("dp", "mp"), 9, ffn_grad
+    )
     ffn_grad = ffn_grad.reshape(dp, share, 3, units)[..., :real_units].transpose(2, 1, 0, 3)
     ffn_grad = ffn_grad.reshape(3, share, dp * real_units).astype(full)
 

time: 474 us -> 421 us (0.89)
  Pallas kernels: 313 us -> 294 us
  between operations: 15.9 us -> 2.37 us
  other arithmetic: 31.4 us -> 20.7 us
  local copies, waits for them, and re-layouts: 69.3 us -> 58.7 us
    pallas_call x11 -> x10, Pallas kernels: 313 us -> 294 us  [the longest x5 151 us: gather(): pl.pallas_call(functools.partial(gather_kernel, dims, chunks, firsts, par...]
    reshape x6, local copies, waits for them, and re-layouts: 6.14 us -> 0.54 us  [on_device(): g.reshape(dp, -1)]
  transfers between devices with their start and end apart: 1 -> 0, of which waited for: 0 -> 0; matrix products, arithmetic and copies ran while one was open for 4% -> 0% of each run, Pallas kernels for 14% -> 0%
where the time goes in v3:
time: 421 us; the launch traced here: 416 us
  Pallas kernels  294 us (70%)
  local copies, waits for them, and re-layouts  58.7 us (14%)
  matrix products  27.1 us (6%)
  other arithmetic  20.7 us (5%)
  blocking collectives  13.7 us (3%)
    pallas_call x5, Pallas kernels, gather(): pl.pallas_call(functools.partial(gather_kernel, dims, chunks, firsts, par...  151 us
    pallas_call x5, Pallas kernels, scatter(): pl.pallas_call(functools.partial(scatter_kernel, dims, chunks, firsts, pa...  143 us
    dot_general x6, matrix products, inner_rows(): lax.dot_general(left_op, right_op, (((0,), (0,)), ((), ())), preferred_el...  10.4 us
    dot_general x2, local copies, waits for them, and re-layouts, inner_rows(): lax.dot_general(left_op, right_op, (((0,), (0,)), ((), ())), preferred_el...  9.58 us
    dot_general x6, matrix products, matmul(): return jnp.dot(left_op, right_op, preferred_element_type=jnp.float32)  9.04 us

profile of v3, /device:TPU:13, one launch (start us, length us, event | category | flops | bytes accessed | tf_op | source)
XLA Modules:
  0.0 416.4 jit_solution(5282523930743263992)
XLA Ops:
  0.6 4.1 concatenate.51
  4.8 1.0 fusion.29.refs_0_
  5.8 46.0 %shard_map.271 = bf16[4,2,160,1024]{3,2,1,0:T(8,128)(2,1)S(1)} custom-call(bf16[160,1024]{1,0:T(8,128)(2,1)S(1)} %fusion.29.refs_0_), custom_call_target="tpu_custom_call" | custom-call | bytes 52428800 | tf_op jit(solution)/shard_map/pallas_call | solution.py:232
  56.9 1.5 convolution_convert_fusion.4
  58.4 7.7 %shard_map.272 = f32[48,1152]{1,0:T(8,128)S(1)} custom-call(bf16[2,2,48,1152]{3,2,1,0:T(8,128)(2,1)S(1)} %bitcast.72), custom_call_target="tpu_custom_call" | custom-call | bytes 8847360 | tf_op jit(solution)/shard_map/pallas_call | solution.py:346
  67.8 0.9 stack.12
  69.7 1.0 stack.13
  70.7 0.9 copy.64
  71.6 2.0 stack.14
  74.5 4.5 %maximum_bitcast_fusion = bf16[8,144,3,216]{3,2,1,0:T(4,128)(2,1)S(1)} fusion(bf16[1,144,8,216]{3,0,1,2:T(2,128)(2,1)S(1)} %copy.65, bf16[1,144,8,216]{3,0,1,2:T(2,128)(2,1)S(1)} %copy.64, bf16[1,144,8,216]{3,0,1,2:T(2,128)(2,1)S(1)} %copy.63), kind=kLoop, calls=%fused_computation.8 | loop fusion | flops 4478976 | bytes 2985984 | tf_op jit(solution)/shard_map/transpose | solution.py:418
  79.0 2.6 pad.41
  81.6 4.4 %reshape.332.refs_1_ = bf16[8,144,768]{2,1,0:T(8,128)(2,1)S(1)} reshape(bf16[8,144,3,256]{3,2,1,0:T(4,128)(2,1)} %pad.41) | data formatting | bytes 3538944 | tf_op jit(solution)/shard_map/reshape | solution.py:420
  86.1 57.0 %shard_map.273 = (bf16[4,2,2,2,48,1152]{5,4,3,2,1,0:T(8,128)(2,1)S(1)}, bf16[8,144,768]{2,1,0:T(8,128)(2,1)S(1)}) custom-call(bf16[48,1152]{1,0:T(8,128)(2,1)S(1)} %multiply_convert_fusion.2.refs_0_, bf16[8,144,768]{2,1,0:T(8,128)(2,1)S(1)} %reshape.332.refs_1_), custom_call_target="tpu_custom_call" | custom-call | bytes 70778880 | tf_op jit(solution)/shard_map/pallas_call | solution.py:232
  143.1 2.2 fusion.17
  145.9 1.1 copy-done.11
  147.1 1.2 convolution_convert_fusion
  148.3 32.0 %shard_map.274 = f32[48,1152]{1,0:T(8,128)S(1)} custom-call(bf16[4,2,2,2,48,1152]{5,4,3,2,1,0:T(8,128)(2,1)S(1)} %bitcast.62), custom_call_target="tpu_custom_call" | custom-call | bytes 70778880 | tf_op jit(solution)/shard_map/pallas_call | solution.py:346
  182.2 33.1 %shard_map.275 = bf16[4,2,2,2,48,1152]{5,4,3,2,1,0:T(8,128)(2,1)S(1)} custom-call(bf16[48,1152]{1,0:T(8,128)(2,1)S(1)} %get-tuple-element.58.refs_0_), custom_call_target="tpu_custom_call" | custom-call | bytes 70778880 | tf_op jit(solution)/shard_map/pallas_call | solution.py:232
  215.3 4.4 %fusion.6 = (bf16[1536,256]{0,1:T(8,128)(2,1)}, bf16[1536,256]{0,1:T(8,128)(2,1)}) fusion(f32[1536,512]{0,1:T(8,128)S(1)} %copy-done.12, bf16[1536,1152]{1,0:T(8,128)(2,1)S(1)} %bitcast.63, bf16[1152,768]{1,0:T(8,128)(2,1)} %bitcast.76), kind=kOutput, calls=%fused_computation.19 | convolution fusion | flops 915406848 | bytes 8847360 | tf_op jit(solution)/shard_map/dot_general | solution.py:20
  219.6 5.8 %copy.66 = bf16[1152,1536]{1,0:T(8,128)(2,1)} copy(bf16[1152,1536]{0,1:T(8,128)(2,1)} %bitcast.68) | data formatting | bytes 7077888 | tf_op jit(solution)/shard_map/dot_general | solution.py:24
  225.4 5.5 %fusion.12 = bf16[8,144,512]{2,1,0:T(8,128)(2,1)} fusion(bf16[8,144,1536]{2,1,0:T(8,128)(2,1)} %bitcast.84, bf16[1536,256]{0,1:T(8,128)(2,1)} %get-tuple-element.48, bf16[1536,256]{0,1:T(8,128)(2,1)} %get-tuple-element.47), kind=kOutput, calls=%fused_computation.28 | convolution fusion | flops 1815674880 | bytes 6291456 | tf_op jit(solution)/shard_map/dot_general | solution.py:24
  230.9 3.8 copy.68
  234.7 3.4 convolution_convert_fusion.6
  238.3 1.3 copy-done.4
  240.1 2.2 convolution_convert_fusion.1
  242.4 51.6 %shard_map.276 = (f32[48,1152]{1,0:T(8,128)S(1)}, bf16[8,144,768]{2,1,0:T(8,128)(2,1)S(1)}) custom-call(bf16[4,2,2,2,48,1152]{5,4,3,2,1,0:T(8,128)(2,1)S(1)} %bitcast.69, bf16[8,144,768]{2,1,0:T(8,128)(2,1)S(1)} %pad_maximum_fusion.2.refs_1_), custom_call_target="tpu_custom_call" | custom-call | bytes 70778880 | tf_op jit(solution)/shard_map/pallas_call | solution.py:346
  294.3 1.2 multiply_reduce_fusion.1
  295.7 6.6 %shard_map.277 = bf16[2,2,48,1152]{3,2,1,0:T(8,128)(2,1)S(1)} custom-call(bf16[48,1152]{1,0:T(8,128)(2,1)S(1)} %fusion.37.refs_0_), custom_call_target="tpu_custom_call" | custom-call | bytes 8847360 | tf_op jit(solution)/shard_map/pallas_call | solution.py:232
  302.3 1.4 convolution_convert_fusion.7
  306.9 1.6 pad_maximum_fusion.1
  308.6 4.3 %copy.70 = bf16[1152,1024]{1,0:T(8,128)(2,1)} copy(bf16[1152,1024]{0,1:T(8,128)(2,1)} %pad_maximum_fusion.1) | data formatting | bytes 4718592 | tf_op jit(solution)/shard_map/concatenate | solution.py:520
  312.9 2.2 convolution_convert_fusion.5
  315.1 6.3 %shard_map.278 = f32[48,1152]{1,0:T(8,128)S(1)} custom-call(bf16[2,2,48,1152]{3,2,1,0:T(8,128)(2,1)S(1)} %bitcast.73), custom_call_target="tpu_custom_call" | custom-call | bytes 8847360 | tf_op jit(solution)/shard_map/pallas_call | solution.py:346
  322.3 2.0 pad_maximum_fusion.refs_0_
  324.2 45.4 %shard_map.279 = f32[160,1024]{1,0:T(8,128)S(1)} custom-call(bf16[4,2,160,1024]{3,2,1,0:T(8,128)(2,1)S(1)} %pad_maximum_fusion.refs_0_), custom_call_target="tpu_custom_call" | custom-call | bytes 52428800 | tf_op jit(solution)/shard_map/pallas_call | solution.py:346
  369.8 8.3 %shard_map.280 = bf16[2,2,160,512]{3,2,1,0:T(8,128)(2,1)S(1)} custom-call(bf16[160,512]{1,0:T(8,128)(2,1)S(1)} %pad_maximum_fusion.7.refs_0_), custom_call_target="tpu_custom_call" | custom-call | bytes 13107200 | tf_op jit(solution)/shard_map/pallas_call | solution.py:232
  380.9 2.8 reshape.340
  383.7 2.3 convert_bitcast_fusion
  385.9 2.7 fusion.106
  388.7 1.7 copy.74
  390.4 2.7 squeeze.12
  393.1 1.7 copy.72
  394.8 2.7 squeeze.10
  398.2 1.4 squeeze.11
  399.7 1.1 fusion.39
  400.7 6.8 %all_gather.7 = bf16[192,1152]{1,0:T(8,128)(2,1)S(1)} all-gather(bf16[48,1152]{1,0:T(8,128)(2,1)S(1)} %fusion.39), channel_id=1, replica_groups=mesh['dp'=8,'mp'=4] {'mp'}, dimensions={0}, use_global_device_ids=true | all-gather | bytes 552960 | tf_op jit(solution)/shard_map/all_gather | solution.py:533
  407.6 1.0 convert_element_type.151
  408.5 6.8 %all_gather.6 = bf16[192,1152]{1,0:T(8,128)(2,1)S(1)} all-gather(bf16[48,1152]{1,0:T(8,128)(2,1)S(1)} %copy-done.20), channel_id=1, replica_groups=mesh['dp'=8,'mp'=4] {'mp'}, dimensions={0}, use_global_device_ids=true | all-gather | bytes 552960 | tf_op jit(solution)/shard_map/all_gather | solution.py:532
  (232 shorter events, 19.7 us)
Async XLA Ops:
  52.2 1.6 copy-start.10
  53.2 1.8 copy-start.59
  53.9 3.0 copy-start.8
  54.1 4.3 %copy-start.39 = (f32[192]{0:T(256)}, f32[192]{0:T(256)S(1)}, u32[]{:S(2)}) copy-start(f32[192]{0:T(256)S(1)} %fusion.91) | copy-start | bytes 2308
  54.7 3.7 copy-start.41
  54.8 3.6 copy-start.35
  54.9 3.5 copy-start.37
  55.4 3.0 copy-start.45
  56.3 11.3 %copy-start.16 = (f32[192,192]{0,1:T(8,128)}, f32[192,192]{0,1:T(8,128)S(1)}, u32[]{:S(2)}) copy-start(f32[192,192]{0,1:T(8,128)S(1)} %get-tuple-element.85) | copy-start | bytes 442372
  56.3 11.3 %copy-start.55 = (f32[192]{0:T(256)}, f32[192]{0:T(256)S(1)}, u32[]{:S(2)}) copy-start(f32[192]{0:T(256)S(1)} %get-tuple-element.84) | copy-start | bytes 2308
  56.7 10.9 %copy-start.57 = (f32[192]{0:T(256)}, f32[192]{0:T(256)S(1)}, u32[]{:S(2)}) copy-start(f32[192]{0:T(256)S(1)} %fusion.49) | copy-start | bytes 2308
  56.7 11.1 %copy-start.18 = (bf16[144,1728]{1,0:T(8,128)(2,1)S(1)}, bf16[144,1728]{1,0:T(8,128)(2,1)}, u32[]{:S(2)}) copy-start(bf16[144,1728]{1,0:T(8,128)(2,1)} %param.23) | copy-start | bytes 1492996
  56.9 10.9 %copy-start.21 = (bf16[192,256]{1,0:T(8,128)(2,1)}, bf16[192,256]{1,0:T(8,128)(2,1)S(1)}, u32[]{:S(2)}) copy-start(bf16[192,256]{1,0:T(8,128)(2,1)S(1)} %convolution_convert_fusion.9) | copy-start | bytes 294916
  66.1 3.6 copy-start
  66.3 3.4 copy-start.51
  66.8 114.5 %copy-start.43 = (f32[48]{0:T(128)}, f32[48]{0:T(128)S(1)}, u32[]{:S(2)}) copy-start(f32[48]{0:T(128)S(1)} %dynamic_slice.10) | copy-start | bytes 580
  67.6 3.1 copy-start.67
  67.6 113.8 %copy-start.6 = (f32[48,1152]{1,0:T(8,128)}, f32[48,1152]{1,0:T(8,128)S(1)}, u32[]{:S(2)}) copy-start(f32[48,1152]{1,0:T(8,128)S(1)} %get-tuple-element.43) | copy-start | bytes 663556
  67.6 2.1 copy-start.19
  67.6 3.1 copy-start.53
  143.1 2.3 copy-start.2
  143.1 2.8 copy-start.3
  145.4 1.7 copy-start.11
  148.3 32.3 %copy-start.23 = (bf16[192,1152]{1,0:T(8,128)(2,1)S(1)}, bf16[192,1152]{1,0:T(8,128)(2,1)}, u32[]{:S(2)}) copy-start(bf16[192,1152]{1,0:T(8,128)(2,1)} %param.18) | copy-start | bytes 1327108
  182.2 33.1 %copy-start.12 = (f32[1536,512]{0,1:T(8,128)S(1)}, f32[1536,512]{0,1:T(8,128)}, u32[]{:S(2)}) copy-start(f32[1536,512]{0,1:T(8,128)} %copy-done.11) | copy-start | bytes 9437188
  234.7 3.4 copy-start.15
  238.2 1.7 copy-start.69
  238.2 1.9 copy-start.70
  242.3 51.7 %copy-start.7 = (f32[48,1152]{1,0:T(8,128)S(1)}, f32[48,1152]{1,0:T(8,128)}, u32[]{:S(2)}) copy-start(f32[48,1152]{1,0:T(8,128)} %copy-done.6) | copy-start | bytes 663556
  242.3 51.7 %copy-start.54 = (f32[48]{0:T(128)S(1)}, f32[48]{0:T(128)}, u32[]{:S(2)}) copy-start(f32[48]{0:T(128)} %copy-done.53) | copy-start | bytes 580
  242.3 51.9 %copy-start.68 = (f32[48]{0:T(128)S(1)}, f32[48]{0:T(128)}, u32[]{:S(2)}) copy-start(f32[48]{0:T(128)} %copy-done.67) | copy-start | bytes 580
  242.4 51.9 %copy-start.1 = (f32[48,1152]{1,0:T(8,128)S(1)}, f32[48,1152]{1,0:T(8,128)}, u32[]{:S(2)}) copy-start(f32[48,1152]{1,0:T(8,128)} %copy-done) | copy-start | bytes 663556
  242.4 51.9 %copy-start.44 = (f32[48]{0:T(128)S(1)}, f32[48]{0:T(128)}, u32[]{:S(2)}) copy-start(f32[48]{0:T(128)} %copy-done.43) | copy-start | bytes 580
  242.4 51.9 %copy-start.52 = (f32[48]{0:T(128)S(1)}, f32[48]{0:T(128)}, u32[]{:S(2)}) copy-start(f32[48]{0:T(128)} %copy-done.51) | copy-start | bytes 580
  242.4 53.1 %copy-start.66 = (f32[48]{0:T(128)S(1)}, f32[48]{0:T(128)}, u32[]{:S(2)}) copy-start(f32[48]{0:T(128)} %copy-done.65) | copy-start | bytes 580
  294.2 9.5 %copy-start.9 = (f32[192,768]{1,0:T(8,128)S(1)}, f32[192,768]{1,0:T(8,128)}, u32[]{:S(2)}) copy-start(f32[192,768]{1,0:T(8,128)} %copy-done.8) | copy-start | bytes 1769476
  294.2 9.5 %copy-start.17 = (f32[192,192]{0,1:T(8,128)S(1)}, f32[192,192]{0,1:T(8,128)}, u32[]{:S(2)}) copy-start(f32[192,192]{0,1:T(8,128)} %copy-done.16) | copy-start | bytes 442372
  294.2 9.5 %copy-start.56 = (f32[192]{0:T(256)S(1)}, f32[192]{0:T(256)}, u32[]{:S(2)}) copy-start(f32[192]{0:T(256)} %copy-done.55) | copy-start | bytes 2308
  294.2 9.5 %copy-start.58 = (f32[192]{0:T(256)S(1)}, f32[192]{0:T(256)}, u32[]{:S(2)}) copy-start(f32[192]{0:T(256)} %copy-done.57) | copy-start | bytes 2308
  295.7 8.4 %copy-start.29 = (bf16[192,128]{1,0:T(8,128)(2,1)S(1)}, bf16[192,128]{1,0:T(8,128)(2,1)}, u32[]{:S(2)}) copy-start(bf16[192,128]{1,0:T(8,128)(2,1)} %copy-done.28) | copy-start | bytes 147460
  295.7 8.4 %copy-start.31 = (bf16[192,128]{1,0:T(8,128)(2,1)S(1)}, bf16[192,128]{1,0:T(8,128)(2,1)}, u32[]{:S(2)}) copy-start(bf16[192,128]{1,0:T(8,128)(2,1)} %copy-done.30) | copy-start | bytes 147460
  295.7 8.6 %copy-start.25 = (bf16[192,128]{1,0:T(8,128)(2,1)S(1)}, bf16[192,128]{1,0:T(8,128)(2,1)}, u32[]{:S(2)}) copy-start(bf16[192,128]{1,0:T(8,128)(2,1)} %copy-done.24) | copy-start | bytes 147460
  295.7 8.6 %copy-start.27 = (bf16[192,128]{1,0:T(8,128)(2,1)S(1)}, bf16[192,128]{1,0:T(8,128)(2,1)}, u32[]{:S(2)}) copy-start(bf16[192,128]{1,0:T(8,128)(2,1)} %copy-done.26) | copy-start | bytes 147460
  302.3 2.2 copy-start.46
  302.3 2.2 copy-start.61
  312.8 8.5 %copy-start.64 = (f32[48]{0:T(128)S(1)}, f32[48]{0:T(128)}, u32[]{:S(2)}) copy-start(f32[48]{0:T(128)} %get-tuple-element.55) | copy-start | bytes 580
  312.8 9.2 %copy-start.34 = (bf16[1152]{0:T(1024)(128)(2,1)S(1)}, bf16[1152]{0:T(1024)(128)(2,1)}, u32[]{:S(2)}) copy-start(bf16[1152]{0:T(1024)(128)(2,1)} %get-tuple-element.27) | copy-start | bytes 6916
  399.6 8.9 %copy-start.20 = (bf16[48,1152]{1,0:T(8,128)(2,1)S(1)}, bf16[48,1152]{1,0:T(8,128)(2,1)}, u32[]{:S(2)}) copy-start(bf16[48,1152]{1,0:T(8,128)(2,1)} %get-tuple-element.59) | copy-start | bytes 331780
  (23 other events, 23.4 us)
